TPU v7x, 512 devices: a whole 4x8x8 slice. The times are simulated.
512 devices in a mesh: fsdp: 16 (over z, core), tp: 32 (over y, x).
Axes of the slice: x: 4, y: 8, z: 8, core: 2. Of those that a mesh axis runs over, the one named last changes fastest.
Arguments:
- momentum: bfloat16 [8192, 14336], P('fsdp', 'tp'), may hold values from -6 to 6
- grad: bfloat16 [8192, 14336], P('fsdp', 'tp'), may hold values from -80 to 80
- basis: bfloat16 [14336, 1024], P('tp', 'fsdp'), may hold values from -6 to 6
Outputs:
- momentum_new: bfloat16 [8192, 14336], P('fsdp', 'tp')
- basis_new: bfloat16 [14336, 1024], P('tp', 'fsdp')
- update: bfloat16 [8192, 14336], P('fsdp', 'tp')
All inputs are finite; a program needn't handle non-finite values.
Results may differ from a plain program's by a relative error of at most 0.018.
Values may be sent and summed in bfloat16 or wider, within the bound.
No kernel may reach another device: no remote copies, remote signals or barrier semaphores. Data moves between devices by JAX's collectives and lax.ppermute only.
A program may use at most 64 MiB of HBM per device.

v0:
```python
import math

import jax
import jax.numpy as jnp
from jax import lax
from jax.sharding import PartitionSpec as P

keep_rate = 0.95
epsilon = 1e-06


def orthonormal(left, gram):
    chol = jnp.linalg.cholesky(gram)
    return lax.linalg.triangular_solve(chol, left, left_side=False, lower=True, transpose_a=True)


def per_device(momentum, grad, basis):
    share = basis.shape[1]
    rank_all = share * lax.axis_size("fsdp")
    rows_all = momentum.shape[0] * lax.axis_size("fsdp")
    cols_all = momentum.shape[1] * lax.axis_size("tp")
    total = momentum.astype(jnp.float32) + grad.astype(jnp.float32)
    total_b = total.astype(jnp.bfloat16)
    basis_all = lax.all_gather(basis, "fsdp", axis=1, tiled=True)
    block = total_b
    left_part = lax.psum_scatter(
        jnp.dot(block, basis_all, preferred_element_type=jnp.float32),
        "tp",
        scatter_dimension=0,
        tiled=True,
    )
    left = lax.all_gather(left_part, "tp", axis=0, tiled=True)
    gram = lax.psum(jnp.dot(left.T, left, precision=lax.Precision.HIGHEST), "fsdp")
    ortho_b = orthonormal(left, gram).astype(jnp.bfloat16)
    block = total_b
    right_own = lax.psum_scatter(
        lax.dot_general(
            block, ortho_b, (((0,), (0,)), ((), ())), preferred_element_type=jnp.float32
        ).astype(jnp.bfloat16),
        "fsdp",
        scatter_dimension=0,
        tiled=True,
    ).astype(jnp.float32)
    pieces = lax.all_gather(
        jnp.sum(right_own * right_own, axis=0)[None, :], ("fsdp", "tp"), axis=0, tiled=True
    )
    squares = jnp.sum(pieces, axis=0)
    scale = jnp.sqrt(squares / cols_all + epsilon)
    basis_own = (right_own / scale[None, :]).astype(jnp.bfloat16)
    right_b, basis_full = (
        lax.all_gather(right_own.astype(jnp.bfloat16), "fsdp", axis=0, tiled=True),
        lax.all_gather(basis_own, "fsdp", axis=0, tiled=True),
    )
    basis_new = lax.dynamic_slice_in_dim(basis_full, lax.axis_index("fsdp") * share, share, 1)
    correction = lax.dot_general(
        ortho_b, right_b, (((1,), (1,)), ((), ())), preferred_element_type=jnp.float32
    )
    raw = lax.dot_general(
        ortho_b, basis_full, (((1,), (1,)), ((), ())), preferred_element_type=jnp.float32
    )
    momentum_new = (total - (1.0 - keep_rate) * correction).astype(jnp.bfloat16)
    update = (math.sqrt(rows_all / rank_all) * raw).astype(jnp.bfloat16)
    return (momentum_new, basis_new, update)


def solution(mesh):
    return jax.shard_map(
        per_device,
        mesh=mesh,
        in_specs=(P("fsdp", "tp"), P("fsdp", "tp"), P("tp", "fsdp")),
        out_specs=(P("fsdp", "tp"), P("tp", "fsdp"), P("fsdp", "tp")),
        check_vma=False,
    )
```

profile of v0, /device:TPU:1, one launch (start us, length us, event | category | flops | bytes accessed | tf_op | source)
XLA Modules:
  0.0 1011.4 jit_solution(10648312283072700821)
XLA Ops:
  7.2 27.7 %all_gather.15 = bf16[448,1024]{0,1:T(8,128)(2,1)S(1)} all-gather(bf16[448,64]{0,1:T(8,128)(2,1)} %param.5), channel_id=1, replica_groups=mesh['fsdp'=16,'tp'=32] {'fsdp'}, dimensions={1}, use_global_device_ids=true | all-gather | bytes 974848 | tf_op jit(solution)/shard_map/all_gather | solution.py:24
  34.9 3.3 fusion.46
  38.3 212.8 %reduce-scatter.4.cloned.1.call-done = f32[16,1024]{1,0:T(8,128)} async-done(((f32[512,1024]{1,0:T(8,128)}), f32[16,1024]{1,0:T(8,128)}) %reduce-scatter.4.cloned.1.call-update) | async-done | bytes 65552 | tf_op jit(solution)/shard_map/reduce_scatter | solution.py:26
  251.2 86.8 %all-gather.6.cloned.1.call-done = f32[512,1024]{1,0:T(8,128)} async-done(((f32[16,1024]{1,0:T(8,128)}), f32[512,1024]{1,0:T(8,128)}) %all-gather.6.cloned.1.call-update) | async-done | bytes 2097168 | tf_op jit(solution)/shard_map/all_gather | solution.py:32
  338.0 10.3 %fusion.74 = f32[1024,1024]{0,1:T(8,128)} fusion(f32[512,1024]{1,0:T(8,128)} %all-gather.6.cloned.1.call-done), kind=kOutput, calls=%fused_computation.173 | convolution fusion | flops 6442450944 | bytes 6291456 | tf_op jit(solution)/shard_map/dot_general | solution.py:33
  348.4 128.3 %all-reduce.5.cloned.1.call-done = f32[1024,1024]{0,1:T(8,128)} async-done(((f32[1024,1024]{0,1:T(8,128)}), f32[1024,1024]{0,1:T(8,128)}) %all-reduce.5.cloned.1.call-update) | async-done | bytes 4194320 | tf_op jit(solution)/shard_map/psum | solution.py:33
  476.7 5.5 copy.16
  482.2 4.4 fusion.1
  488.6 11.7 %cholesky.223 = f32[128,128]{1,0:T(8,128)S(1)} custom-call(f32[128,128]{1,0:T(8,128)S(1)} %cholesky.580), custom_call_target="Cholesky" | custom-call | tf_op jit(solution)/shard_map/jit(cholesky)/cholesky | solution.py:13
  500.3 9.8 custom-call.62
  510.1 2.5 cholesky.255
  512.6 2.4 constant_dynamic-update-slice_fusion.25
  516.6 11.9 %cholesky.244 = f32[128,128]{1,0:T(8,128)S(1)} custom-call(f32[128,128]{1,0:T(8,128)S(1)} %cholesky.584), custom_call_target="Cholesky" | custom-call | tf_op jit(solution)/shard_map/jit(cholesky)/cholesky | solution.py:13
  529.1 9.8 custom-call.63
  542.3 11.7 %cholesky.468 = f32[128,128]{1,0:T(8,128)S(1)} custom-call(f32[128,128]{1,0:T(8,128)S(1)} %cholesky.589), custom_call_target="Cholesky" | custom-call | tf_op jit(solution)/shard_map/jit(cholesky)/cholesky | solution.py:13
  555.3 9.8 custom-call.64
  566.3 2.3 convolution_subtract_fusion.2
  568.7 12.1 %cholesky.487 = f32[128,128]{1,0:T(8,128)S(1)} custom-call(f32[128,128]{1,0:T(8,128)S(1)} %cholesky.594), custom_call_target="Cholesky" | custom-call | tf_op jit(solution)/shard_map/jit(cholesky)/cholesky | solution.py:13
  582.0 9.8 custom-call.65
  592.9 2.3 convolution_subtract_fusion.10
  595.3 11.7 %cholesky.506 = f32[128,128]{1,0:T(8,128)S(1)} custom-call(f32[128,128]{1,0:T(8,128)S(1)} %cholesky.599), custom_call_target="Cholesky" | custom-call | tf_op jit(solution)/shard_map/jit(cholesky)/cholesky | solution.py:13
  608.3 9.9 custom-call.66
  621.6 11.7 %cholesky.526 = f32[128,128]{1,0:T(8,128)S(1)} custom-call(f32[128,128]{1,0:T(8,128)S(1)} %cholesky.604), custom_call_target="Cholesky" | custom-call | tf_op jit(solution)/shard_map/jit(cholesky)/cholesky | solution.py:13
  634.6 9.8 custom-call.67
  647.4 11.9 %cholesky.546 = f32[128,128]{1,0:T(8,128)S(1)} custom-call(f32[128,128]{1,0:T(8,128)S(1)} %cholesky.609), custom_call_target="Cholesky" | custom-call | tf_op jit(solution)/shard_map/jit(cholesky)/cholesky | solution.py:13
  660.6 9.8 custom-call.68
  673.0 11.7 %cholesky.564 = f32[128,128]{1,0:T(8,128)S(1)} custom-call(f32[128,128]{1,0:T(8,128)S(1)} %convolution_subtract_fusion.13), custom_call_target="Cholesky" | custom-call | tf_op jit(solution)/shard_map/jit(cholesky)/cholesky | solution.py:13
  691.9 4.9 select_select_fusion
  696.8 23.2 %while.1 = (s32[]{:T(128)}, f32[1024,1024]{1,0:T(8,128)}, s32[8,2]{0,1:T(2,128)S(1)}, f32[8,128,128]{2,1,0:T(8,128)S(1)}, s32[]{:T(128)}) while((s32[]{:T(128)}, f32[1024,1024]{1,0:T(8,128)}, s32[8,2]{0,1:T(2,128)S(1)}, f32[8,128,128]{2,1,0:T(8,128)S(1)}, s32[]{:T(128)}) %tuple.60), condition=%wide.while_cond, body=%wide.while_body.sunk | while | flops 2 | bytes 131181 | solution.py:14
  697.4 2.3 bitcast_dynamic-update-slice_fusion.2
  700.3 2.3 bitcast_dynamic-update-slice_fusion.2
  703.2 2.3 bitcast_dynamic-update-slice_fusion.2
  706.2 2.3 bitcast_dynamic-update-slice_fusion.2
  709.1 2.3 bitcast_dynamic-update-slice_fusion.2
  712.0 2.3 bitcast_dynamic-update-slice_fusion.2
  714.9 2.3 bitcast_dynamic-update-slice_fusion.2
  720.0 79.0 %custom-call.69 = f32[8,128,128]{1,2,0:T(8,128)S(1)} custom-call(f32[8,128,128]{2,1,0:T(8,128)S(1)} %get-tuple-element.10), custom_call_target="InvertDiagBlocksLowerTriangular" | custom-call | tf_op jit(solution)/shard_map/triangular_solve | solution.py:14
  803.7 2.4 convolution_subtract_fusion.8
  806.6 2.8 convolution_subtract_fusion.9
  810.1 3.2 convolution_subtract_fusion.4
  813.9 3.6 convolution_subtract_fusion.7
  818.1 4.1 convolution_subtract_fusion.3
  824.3 29.6 %fusion = bf16[32,1024]{1,0:T(8,128)(2,1)S(1)} fusion(bf16[448,1024]{1,0:T(8,128)(2,1)S(1)} %convolution_convert_fusion), kind=kCustom, calls=%all-reduce-scatter | all-reduce-scatter fusion | flops 524289 | bytes 985088
  853.9 3.2 collective-permute-start
  861.4 22.1 %all-gather.1 = bf16[16,28,1024]{2,1,0:T(8,128)(2,1)S(1)} all-gather(bf16[1,28,1024]{2,1,0:T(8,128)(2,1)S(1)} %dynamic-slice_bitcast_fusion), channel_id=1, replica_groups=mesh['fsdp'=16,'tp'=32] {'fsdp'}, dimensions={0}, use_global_device_ids=true | all-gather | bytes 974848 | tf_op jit(solution)/shard_map/all_gather | solution.py:51
  883.7 2.6 fusion.4
  886.4 94.9 %all-gather.8.cloned.1.call-done = f32[524288]{0:T(1024)} async-done(((f32[1024]{0:T(1024)}), f32[524288]{0:T(1024)}) %all-gather.8.cloned.1.call-update) | async-done | bytes 2097168 | tf_op jit(solution)/shard_map/all_gather | solution.py:44
  983.1 19.1 %all-gather.2 = bf16[16,28,1024]{2,1,0:T(8,128)(2,1)S(1)} all-gather(bf16[1,28,1024]{2,1,0:T(8,128)(2,1)S(1)} %fusion.53), channel_id=1, replica_groups=mesh['fsdp'=16,'tp'=32] {'fsdp'}, dimensions={0}, use_global_device_ids=true | all-gather | bytes 974848 | tf_op jit(solution)/shard_map/all_gather | solution.py:52
  (108 shorter events, 51.6 us)
Async XLA Ops:
  7.2 243.9 %reduce-scatter.4.cloned.1.call-start = ((), (), s32[]{:S(2)}) async-start(), calls=%async_computation.1 | async-start | bytes 2162688 | tf_op jit(solution)/shard_map/reduce_scatter | solution.py:26
  38.2 299.7 %all-gather.6.cloned.1.call-start = ((), (), s32[]{:S(2)}) async-start(), calls=%async_computation.2 | async-start | bytes 2162688 | tf_op jit(solution)/shard_map/all_gather | solution.py:32
  251.1 225.6 %all-reduce.5.cloned.1.call-start = ((), (), s32[]{:S(2)}) async-start(), calls=%async_computation.3 | async-start | bytes 8388608 | tf_op jit(solution)/shard_map/psum | solution.py:33
  348.3 632.9 %all-gather.8.cloned.1.call-start = ((), (), s32[]{:S(2)}) async-start(), calls=%async_computation.4 | async-start | bytes 2101248 | tf_op jit(solution)/shard_map/all_gather | solution.py:44
  486.6 1.9 copy-start.1
  691.9 107.2 %copy-start = (f32[512,1024]{1,0:T(8,128)S(1)}, f32[512,1024]{1,0:T(8,128)}, u32[]{:S(2)}) copy-start(f32[512,1024]{1,0:T(8,128)} %all-gather.6.cloned.1.call-done) | copy-start | bytes 6291460
  813.4 10.2 %copy-start.2 = (bf16[512,448]{0,1:T(8,128)(2,1)S(1)}, bf16[512,448]{0,1:T(8,128)(2,1)}, u32[]{:S(2)}) copy-start(bf16[512,448]{0,1:T(8,128)(2,1)} %param.4) | copy-start | bytes 1376260
  813.4 10.2 %copy-start.3 = (bf16[512,448]{0,1:T(8,128)(2,1)S(1)}, bf16[512,448]{0,1:T(8,128)(2,1)}, u32[]{:S(2)}) copy-start(bf16[512,448]{0,1:T(8,128)(2,1)} %param.3) | copy-start | bytes 1376260
  822.6 1.0 copy-start.4
  853.9 6.4 collective-permute-start
  857.1 3.2 collective-permute-start.1
  886.4 116.1 %copy-start.5 = (bf16[512,1024]{0,1:T(8,128)(2,1)S(1)}, bf16[512,1024]{0,1:T(8,128)(2,1)}, u32[]{:S(2)}) copy-start(bf16[512,1024]{0,1:T(8,128)(2,1)} %copy-done.4) | copy-start | bytes 3145732
Sparse Core Ops, SparseCore 0:
  38.4 212.6 reduce-scatter.3
  254.7 83.2 all-gather.5
  348.5 128.1 all-reduce.4
  861.5 119.6 all-gather.7
where the time goes:
time: 1020 us; the launch traced here: 1010 us
  waiting for transfers between devices  523 us (51%)
  other arithmetic  262 us (26%)
  blocking collectives  98.5 us (10%)
  matrix products  64.3 us (6%)
  local copies, waits for them, and re-layouts  39.1 us (4%)
  between operations  20.2 us (2%)
    reduce_scatter x1, waiting for transfers between devices, per_device(): lax.psum_scatter(jnp.dot(block, basis_all, preferred_element_type=jnp.flo...  213 us
    another operation x30, other arithmetic, orthonormal(): chol = jnp.linalg.cholesky(gram)  172 us
    psum x1, waiting for transfers between devices, per_device(): lax.psum(jnp.dot(left.T, left, precision=lax.Precision.HIGHEST), 'fsdp')  128 us
    all_gather x1, waiting for transfers between devices, per_device(): lax.all_gather(jnp.sum(right_own * right_own, axis=0)[None, :], ('fsdp',...  94.9 us
    all_gather x1, waiting for transfers between devices, per_device(): left = lax.all_gather(left_part, 'tp', axis=0, tiled=True)  86.8 us
    another operation x3, other arithmetic, orthonormal(): lax.linalg.triangular_solve(chol, left, left_side=False, lower=True, tran...  83.9 us
    unnamed x1, blocking collectives  29.6 us
    all_gather x1, blocking collectives, per_device(): basis_all = lax.all_gather(basis, 'fsdp', axis=1, tiled=True)  27.7 us
  transfers between devices with their start and end apart: 6, of which 4 were waited for; matrix products, arithmetic and copies ran while one was open for 0% of the time, Pallas kernels for 0%

commit v1 on v0

v1 whole, which is shorter than its diff:
```python
import math

import jax
import jax.numpy as jnp
from jax import lax
from jax.sharding import PartitionSpec as P

keep_rate = 0.95
epsilon = 1e-06


def groups(n_fsdp):
    z_groups = [[2 * z + c for z in range(n_fsdp // 2)] for c in range(2)]
    core_groups = [[2 * z, 2 * z + 1] for z in range(n_fsdp // 2)]
    return z_groups, core_groups


def exchange(pieces, axis, index_groups=None):
    return lax.all_to_all(pieces, axis, 0, 0, tiled=True, axis_index_groups=index_groups)


def collect(own, axis, count, index_groups=None):
    copies = jnp.broadcast_to(own[None], (count,) + own.shape)
    return exchange(copies, axis, index_groups)


def split_parts(value):
    high = value.astype(jnp.bfloat16)
    low = (value - high.astype(jnp.float32)).astype(jnp.bfloat16)
    return high, low


def per_device(momentum, grad, basis):
    n_fsdp, n_tp = lax.axis_size("fsdp"), lax.axis_size("tp")
    n_z = n_fsdp // 2
    z_groups, core_groups = groups(n_fsdp)
    rows, cols = momentum.shape
    share = basis.shape[1]
    rank = share * n_fsdp
    rows_all, cols_all = rows * n_fsdp, cols * n_tp
    me_fsdp, me_tp = lax.axis_index("fsdp"), lax.axis_index("tp")

    total = momentum.astype(jnp.float32) + grad.astype(jnp.float32)
    total_b = total.astype(jnp.bfloat16)
    basis_all = lax.all_gather(basis, "fsdp", axis=1, tiled=True)
    part = jnp.dot(total_b, basis_all, preferred_element_type=jnp.float32)
    left_own = jnp.sum(exchange(part.reshape(n_tp, rows // n_tp, rank), "tp"), axis=0)
    left = collect(left_own, "tp", n_tp).reshape(rows, rank)

    slab = rank // n_tp
    mine = lax.dynamic_slice_in_dim(left, me_tp * slab, slab, 1)
    gram_part = lax.dot_general(
        mine, left, (((0,), (0,)), ((), ())), precision=lax.Precision.HIGHEST
    )
    half = jnp.sum(
        exchange(gram_part.reshape(2, slab // 2, rank), "fsdp", core_groups), axis=0
    )
    half = jnp.sum(collect(half, "fsdp", n_z, z_groups), axis=0)
    own_half = collect(half, "tp", n_tp)
    other_half = lax.ppermute(own_half, "fsdp", [(i, i ^ 1) for i in range(n_fsdp)])
    first = (me_fsdp % 2) == 0
    gram = jnp.stack(
        [jnp.where(first, own_half, other_half), jnp.where(first, other_half, own_half)], axis=1
    ).reshape(rank, rank)

    high, low = split_parts(left)
    dims = (((0,), (0,)), ((), ()))
    back = lax.dot_general(total_b, high, dims, preferred_element_type=jnp.float32)
    back = back + lax.dot_general(total_b, low, dims, preferred_element_type=jnp.float32)
    padded = -(-cols // (8 * n_fsdp)) * 8 * n_fsdp
    back = jnp.pad(back, ((0, padded - cols), (0, 0)))
    back = lax.psum_scatter(back, "fsdp", scatter_dimension=0, tiled=True)
    back = lax.all_gather(back, "fsdp", axis=0, tiled=True)[:cols]

    chol = jnp.linalg.cholesky(gram)
    solved = lax.linalg.triangular_solve(
        chol, jnp.concatenate([left, back]), left_side=False, lower=True, transpose_a=True
    )
    ortho_b = solved[:rows].astype(jnp.bfloat16)
    right = solved[rows:]
    squares = collect(jnp.sum(right * right, axis=0)[None], "tp", n_tp)
    scale = jnp.sqrt(jnp.sum(squares, axis=(0, 1)) / cols_all + epsilon)
    right_b = right.astype(jnp.bfloat16)
    basis_full = (right / scale[None, :]).astype(jnp.bfloat16)
    basis_new = lax.dynamic_slice_in_dim(basis_full, me_fsdp * share, share, 1)
    correction = lax.dot_general(
        ortho_b, right_b, (((1,), (1,)), ((), ())), preferred_element_type=jnp.float32
    )
    raw = lax.dot_general(
        ortho_b, basis_full, (((1,), (1,)), ((), ())), preferred_element_type=jnp.float32
    )
    momentum_new = (total - (1.0 - keep_rate) * correction).astype(jnp.bfloat16)
    update = (math.sqrt(rows_all / rank) * raw).astype(jnp.bfloat16)
    return (momentum_new, basis_new, update)


def solution(mesh):
    return jax.shard_map(
        per_device,
        mesh=mesh,
        in_specs=(P("fsdp", "tp"), P("fsdp", "tp"), P("tp", "fsdp")),
        out_specs=(P("fsdp", "tp"), P("tp", "fsdp"), P("fsdp", "tp")),
        check_vma=False,
    )
```

time: 1020 us -> 656 us (0.64)
  waiting for transfers between devices: 523 us -> 107 us
  starting transfers between devices: 4.61 us -> 26.6 us
  blocking collectives: 98.5 us -> 114 us
  local copies, waits for them, and re-layouts: 39.1 us -> 49.5 us
    reduce_scatter x1, waiting for transfers between devices: 213 us -> 7.98 us  [per_device(): back = lax.psum_scatter(back, 'fsdp', scatter_dimension=0, tiled=True)]
    all_gather x2 -> x1, waiting for transfers between devices: 182 us -> 0.02 us  [per_device(): back = lax.all_gather(back, 'fsdp', axis=0, tiled=True)[:cols]]
    psum x1 -> x0, waiting for transfers between devices: 128 us -> none  [per_device(): lax.psum(jnp.dot(left.T, left, precision=lax.Precision.HIGHEST), 'fsdp')]
    all_to_all x0 -> x3, waiting for transfers between devices: none -> 98.9 us  [exchange(): lax.all_to_all(pieces, axis, 0, 0, tiled=True, axis_index_groups=index_gr...]
    all_to_all x0 -> x3, blocking collectives: none -> 86.4 us  [exchange(): lax.all_to_all(pieces, axis, 0, 0, tiled=True, axis_index_groups=index_gr...]
    all_gather x2 -> x0, blocking collectives: 41.2 us -> none  [the longest x1 22.1 us: per_device(): lax.all_gather(right_own.astype(jnp.bfloat16), 'fsdp', axis=0, tiled=True)]
    unnamed x1 -> x0, blocking collectives: 29.6 us -> none
    all_to_all x0 -> x3, starting transfers between devices: none -> 21.9 us  [exchange(): lax.all_to_all(pieces, axis, 0, 0, tiled=True, axis_index_groups=index_gr...]
  transfers between devices with their start and end apart: 6 -> 6, of which waited for: 4 -> 4; matrix products, arithmetic and copies ran while one was open for 0% -> 52% of each run, Pallas kernels for 0% -> 0%
where the time goes in v1:
time: 656 us; the launch traced here: 647 us
  other arithmetic  272 us (41%)
  blocking collectives  114 us (17%)
  waiting for transfers between devices  107 us (16%)
  matrix products  57.9 us (9%)
  local copies, waits for them, and re-layouts  49.5 us (8%)
  starting transfers between devices  26.6 us (4%)
  between operations  19.9 us (3%)
    another operation x30, other arithmetic, per_device(): chol = jnp.linalg.cholesky(gram)  174 us
    all_to_all x3, waiting for transfers between devices, exchange(): lax.all_to_all(pieces, axis, 0, 0, tiled=True, axis_index_groups=index_gr...  98.9 us
    all_to_all x3, blocking collectives, exchange(): lax.all_to_all(pieces, axis, 0, 0, tiled=True, axis_index_groups=index_gr...  86.4 us
    another operation x3, other arithmetic, per_device(): lax.linalg.triangular_solve(chol, jnp.concatenate([left, back]), left_sid...  84.6 us
    another operation x24, local copies, waits for them, and re-layouts  28 us
    all_gather x1, blocking collectives, per_device(): basis_all = lax.all_gather(basis, 'fsdp', axis=1, tiled=True)  27.7 us
    another operation x15, matrix products, per_device(): lax.linalg.triangular_solve(chol, jnp.concatenate([left, back]), left_sid...  23.6 us
    another operation x14, matrix products, per_device(): chol = jnp.linalg.cholesky(gram)  23.1 us
  transfers between devices with their start and end apart: 6, of which 4 were waited for; matrix products, arithmetic and copies ran while one was open for 52% of the time, Pallas kernels for 0%

profile of v1, /device:TPU:1, one launch (start us, length us, event | category | flops | bytes accessed | tf_op | source)
XLA Modules:
  0.0 647.1 jit_solution(13115820231785377102)
XLA Ops:
  7.2 27.7 %all_gather.6 = bf16[448,1024]{0,1:T(8,128)(2,1)S(1)} all-gather(bf16[448,64]{0,1:T(8,128)(2,1)} %param.5), channel_id=1, replica_groups=mesh['fsdp'=16,'tp'=32] {'fsdp'}, dimensions={1}, use_global_device_ids=true | all-gather | bytes 974848 | tf_op jit(solution)/shard_map/all_gather | solution.py:45
  36.8 59.1 %all_to_all.30 = f32[32,16,1024]{2,1,0:T(8,128)} all-to-all(f32[32,16,1024]{2,1,0:T(8,128)S(1)} %bitcast.133), channel_id=1, replica_groups=mesh['fsdp'=16,'tp'=32] {'tp'}, dimensions={0} | all-to-all | bytes 4194304 | tf_op jit(solution)/shard_map/all_to_all | solution.py:19
  99.3 5.9 all-to-all-start.1
  105.2 47.8 %all-to-all-done.1 = f32[32,16,1024]{2,1,0:T(8,128)S(1)} async-done(((f32[32,16,1024]{2,1,0:T(8,128)}), f32[32,16,1024]{2,1,0:T(8,128)S(1)}, u32[]{:S(2)}, u32[]{:S(2)}) %all-to-all-start.1) | async-done | bytes 2097184 | tf_op jit(solution)/shard_map/all_to_all | solution.py:19
  154.5 6.8 %all_to_all.31 = f32[2,16,1024]{2,1,0:T(8,128)S(1)} all-to-all(f32[2,16,1024]{2,1,0:T(8,128)S(1)} %fusion.106), channel_id=1, replica_groups={{0,32},{64,96},{128,160},{192,224},{256,288},{320,352},{384,416},{448,4..., dimensions={0} | all-to-all | bytes 262144 | tf_op jit(solution)/shard_map/all_to_all | solution.py:19
  161.4 20.5 %all_to_all.32 = f32[8,16,1024]{2,1,0:T(8,128)S(1)} all-to-all(f32[8,16,1024]{2,1,0:T(8,128)S(1)} %broadcast_in_dim.10), channel_id=1, replica_groups={{0,64,128,192,256,320,384,448},{32,96,160,224,288,352,416,480},{1,65,12..., dimensions={0} | all-to-all | bytes 1048576 | tf_op jit(solution)/shard_map/all_to_all | solution.py:19
  184.9 5.8 all-to-all-start.4
  193.8 45.3 %all-to-all-done.4 = f32[32,16,1024]{2,1,0:T(8,128)} async-done(((f32[32,16,1024]{2,1,0:T(8,128)}), f32[32,16,1024]{2,1,0:T(8,128)}, u32[]{:S(2)}, u32[]{:S(2)}) %all-to-all-start.4) | async-done | bytes 2097184 | tf_op jit(solution)/shard_map/all_to_all | solution.py:19
  239.1 4.6 collective-permute-start
  243.8 8.0 %reduce-scatter.2.cloned.1.call-done = f32[32,1024]{1,0:T(8,128)} async-done(((f32[512,1024]{1,0:T(8,128)}), f32[32,1024]{1,0:T(8,128)}) %reduce-scatter.2.cloned.1.call-update) | async-done | bytes 131088 | tf_op jit(solution)/shard_map/reduce_scatter | solution.py:72
  251.8 2.7 select_bitcast_fusion.1
  256.7 5.5 copy.20
  262.2 4.4 fusion
  268.6 11.7 %cholesky.223 = f32[128,128]{1,0:T(8,128)S(1)} custom-call(f32[128,128]{1,0:T(8,128)S(1)} %cholesky.580), custom_call_target="Cholesky" | custom-call | tf_op jit(solution)/shard_map/jit(cholesky)/cholesky | solution.py:75
  280.3 2.5 cholesky.255
  282.8 9.8 %custom-call.62 = f32[1,128,128]{1,2,0:T(8,128)S(1)} custom-call(f32[1,128,128]{2,1,0:T(8,128)S(1)} %get-tuple-element.81), custom_call_target="InvertDiagBlocksLowerTriangular" | custom-call | tf_op jit(solution)/shard_map/jit(cholesky)/cholesky | solution.py:75
  297.2 12.7 %cholesky.244 = f32[128,128]{1,0:T(8,128)S(1)} custom-call(f32[128,128]{1,0:T(8,128)} %cholesky.584), custom_call_target="Cholesky" | custom-call | tf_op jit(solution)/shard_map/jit(cholesky)/cholesky | solution.py:75
  310.6 10.6 %custom-call.63 = f32[1,128,128]{1,2,0:T(8,128)S(1)} custom-call(f32[1,128,128]{2,1,0:T(8,128)} %get-tuple-element.78), custom_call_target="InvertDiagBlocksLowerTriangular" | custom-call | tf_op jit(solution)/shard_map/jit(cholesky)/cholesky | solution.py:75
  324.6 11.7 %cholesky.468 = f32[128,128]{1,0:T(8,128)S(1)} custom-call(f32[128,128]{1,0:T(8,128)S(1)} %cholesky.589), custom_call_target="Cholesky" | custom-call | tf_op jit(solution)/shard_map/jit(cholesky)/cholesky | solution.py:75
  337.6 9.8 %custom-call.64 = f32[1,128,128]{1,2,0:T(8,128)S(1)} custom-call(f32[1,128,128]{2,1,0:T(8,128)S(1)} %get-tuple-element.75), custom_call_target="InvertDiagBlocksLowerTriangular" | custom-call | tf_op jit(solution)/shard_map/jit(cholesky)/cholesky | solution.py:75
  351.0 12.1 %cholesky.487 = f32[128,128]{1,0:T(8,128)S(1)} custom-call(f32[128,128]{1,0:T(8,128)S(1)} %cholesky.594), custom_call_target="Cholesky" | custom-call | tf_op jit(solution)/shard_map/jit(cholesky)/cholesky | solution.py:75
  363.7 9.8 %custom-call.65 = f32[1,128,128]{1,2,0:T(8,128)S(1)} custom-call(f32[1,128,128]{2,1,0:T(8,128)S(1)} %get-tuple-element.72), custom_call_target="InvertDiagBlocksLowerTriangular" | custom-call | tf_op jit(solution)/shard_map/jit(cholesky)/cholesky | solution.py:75
  377.0 11.7 %cholesky.506 = f32[128,128]{1,0:T(8,128)S(1)} custom-call(f32[128,128]{1,0:T(8,128)S(1)} %cholesky.599), custom_call_target="Cholesky" | custom-call | tf_op jit(solution)/shard_map/jit(cholesky)/cholesky | solution.py:75
  389.3 10.0 %custom-call.66 = f32[1,128,128]{1,2,0:T(8,128)S(1)} custom-call(f32[1,128,128]{2,1,0:T(8,128)S(1)} %get-tuple-element.69), custom_call_target="InvertDiagBlocksLowerTriangular" | custom-call | tf_op jit(solution)/shard_map/jit(cholesky)/cholesky | solution.py:75
  402.6 11.7 %cholesky.526 = f32[128,128]{1,0:T(8,128)S(1)} custom-call(f32[128,128]{1,0:T(8,128)S(1)} %cholesky.604), custom_call_target="Cholesky" | custom-call | tf_op jit(solution)/shard_map/jit(cholesky)/cholesky | solution.py:75
  415.0 9.8 %custom-call.67 = f32[1,128,128]{1,2,0:T(8,128)S(1)} custom-call(f32[1,128,128]{2,1,0:T(8,128)S(1)} %get-tuple-element.66), custom_call_target="InvertDiagBlocksLowerTriangular" | custom-call | tf_op jit(solution)/shard_map/jit(cholesky)/cholesky | solution.py:75
  427.8 11.9 %cholesky.546 = f32[128,128]{1,0:T(8,128)S(1)} custom-call(f32[128,128]{1,0:T(8,128)S(1)} %cholesky.609), custom_call_target="Cholesky" | custom-call | tf_op jit(solution)/shard_map/jit(cholesky)/cholesky | solution.py:75
  440.3 9.8 %custom-call.68 = f32[1,128,128]{1,2,0:T(8,128)S(1)} custom-call(f32[1,128,128]{2,1,0:T(8,128)S(1)} %get-tuple-element.63), custom_call_target="InvertDiagBlocksLowerTriangular" | custom-call | tf_op jit(solution)/shard_map/jit(cholesky)/cholesky | solution.py:75
  452.7 11.7 %cholesky.564 = f32[128,128]{1,0:T(8,128)S(1)} custom-call(f32[128,128]{1,0:T(8,128)S(1)} %slice_subtract_fusion.6), custom_call_target="Cholesky" | custom-call | tf_op jit(solution)/shard_map/jit(cholesky)/cholesky | solution.py:75
  474.1 4.8 select_select_fusion
  478.9 28.0 %while.1 = (s32[]{:T(128)}, f32[1024,1024]{1,0:T(8,128)}, s32[8,2]{0,1:T(2,128)S(1)}, f32[8,128,128]{2,1,0:T(8,128)}, s32[]{:T(128)}) while((s32[]{:T(128)}, f32[1024,1024]{1,0:T(8,128)}, s32[8,2]{0,1:T(2,128)S(1)}, f32[8,128,128]{2,1,0:T(8,128)}, s32[]{:T(128)}) %tuple.66), condition=%wide.while_cond, body=%wide.while_body.sunk | while | flops 2 | bytes 132205 | solution.py:76
  479.5 2.9 bitcast_dynamic-update-slice_fusion.2
  483.0 2.9 bitcast_dynamic-update-slice_fusion.2
  486.5 2.9 bitcast_dynamic-update-slice_fusion.2
  490.0 2.9 bitcast_dynamic-update-slice_fusion.2
  493.5 2.9 bitcast_dynamic-update-slice_fusion.2
  497.0 2.9 bitcast_dynamic-update-slice_fusion.2
  500.5 2.9 bitcast_dynamic-update-slice_fusion.2
  504.0 2.8 bitcast_dynamic-update-slice_fusion.2
  506.9 79.8 %custom-call.69 = f32[8,128,128]{1,2,0:T(8,128)S(1)} custom-call(f32[8,128,128]{2,1,0:T(8,128)} %get-tuple-element.10), custom_call_target="InvertDiagBlocksLowerTriangular" | custom-call | tf_op jit(solution)/shard_map/triangular_solve | solution.py:76
  596.2 2.6 fusion.21
  599.5 3.2 convolution_subtract_fusion.2
  603.2 3.6 convolution_subtract_fusion
  607.4 4.1 convolution_subtract_fusion.1
  614.9 10.2 %all-to-all-start.5 = ((f32[32,1,1024]{2,1,0:T(1,128)}), f32[32,1,1024]{2,1,0:T(1,128)S(1)}, u32[]{:S(2)}, u32[]{:S(2)}) async-start(f32[32,1,1024]{2,1,0:T(1,128)} %broadcast_in_dim.12), calls=%async_computation.6 | async-start | bytes 262144 | tf_op jit(solution)/shard_map/all_to_all | solution.py:19
  625.1 3.6 fusion.17
  628.6 5.8 all-to-all-done.5
  636.2 3.0 fusion.16
  (102 shorter events, 71.6 us)
Async XLA Ops:
  99.3 53.7 %all-to-all-start.1 = ((f32[32,16,1024]{2,1,0:T(8,128)}), f32[32,16,1024]{2,1,0:T(8,128)S(1)}, u32[]{:S(2)}, u32[]{:S(2)}) async-start(f32[32,16,1024]{2,1,0:T(8,128)} %broadcast_in_dim.9), calls=%async_computation.1 | async-start | bytes 4194304 | tf_op jit(solution)/shard_map/all_to_all | solution.py:19
  161.4 29.4 %copy-start.2 = (bf16[512,448]{0,1:T(8,128)(2,1)S(1)}, bf16[512,448]{0,1:T(8,128)(2,1)}, u32[]{:S(2)}) copy-start(bf16[512,448]{0,1:T(8,128)(2,1)} %param.4) | copy-start | bytes 1376260
  161.4 29.4 %copy-start.3 = (bf16[512,448]{0,1:T(8,128)(2,1)S(1)}, bf16[512,448]{0,1:T(8,128)(2,1)}, u32[]{:S(2)}) copy-start(bf16[512,448]{0,1:T(8,128)(2,1)} %param.3) | copy-start | bytes 1376260
  184.9 54.1 %all-to-all-start.4 = ((f32[32,16,1024]{2,1,0:T(8,128)}), f32[32,16,1024]{2,1,0:T(8,128)}, u32[]{:S(2)}, u32[]{:S(2)}) async-start(f32[32,16,1024]{2,1,0:T(8,128)} %broadcast_in_dim.11), calls=%async_computation.5 | async-start | bytes 4194304 | tf_op jit(solution)/shard_map/all_to_all | solution.py:19
  190.7 61.0 %reduce-scatter.2.cloned.1.call-start = ((), (), s32[]{:S(2)}) async-start(), calls=%async_computation.7 | async-start | bytes 2228224 | tf_op jit(solution)/shard_map/reduce_scatter | solution.py:72
  193.7 393.0 %all-gather.2.cloned.1.call-start = ((), (), s32[]{:S(2)}) async-start(), calls=%async_computation.8 | async-start | bytes 2228224 | tf_op jit(solution)/shard_map/all_gather | solution.py:73
  239.1 12.7 %collective-permute-start = (f32[32,16,1024]{2,1,0:T(8,128)}, f32[32,16,1024]{2,1,0:T(8,128)}, u32[]{:S(2)}, u32[]{:S(2)}) collective-permute-start(f32[32,16,1024]{2,1,0:T(8,128)} %all-to-all-done.4), channel_id=1, source_target_pairs={{0,32},{32,0},{64,96},{96,64},{128,160},{160,128},{192,224},{224,1... | collective-permute-start | bytes 6291464 | tf_op jit(solution)/shard_map/ppermute | solution.py:60
  266.6 1.9 copy-start.1
  612.1 1.9 copy-start
  614.9 19.6 %all-to-all-start.5 = ((f32[32,1,1024]{2,1,0:T(1,128)}), f32[32,1,1024]{2,1,0:T(1,128)S(1)}, u32[]{:S(2)}, u32[]{:S(2)}) async-start(f32[32,1,1024]{2,1,0:T(1,128)} %broadcast_in_dim.12), calls=%async_computation.6 | async-start | bytes 262144 | tf_op jit(solution)/shard_map/all_to_all | solution.py:19
Sparse Core Ops, SparseCore 0:
  194.4 57.3 reduce-scatter.1
  253.9 45.1 all-gather.1

commit v2 on v1

v2 whole, which is shorter than its diff:
```python
import functools
import math

import jax
import jax.numpy as jnp
from jax import lax
from jax.experimental import pallas as pl
from jax.experimental.pallas import tpu as pltpu
from jax.sharding import PartitionSpec as P

keep_rate = 0.95
epsilon = 1e-06
BLOCK = 128
SUB = 8
HI = lax.Precision.HIGHEST


def groups(n_fsdp):
    z_groups = [[2 * z + c for z in range(n_fsdp // 2)] for c in range(2)]
    core_groups = [[2 * z, 2 * z + 1] for z in range(n_fsdp // 2)]
    return z_groups, core_groups


def exchange(pieces, axis, index_groups=None):
    return lax.all_to_all(pieces, axis, 0, 0, tiled=True, axis_index_groups=index_groups)


def collect(own, axis, count, index_groups=None):
    copies = jnp.broadcast_to(own[None], (count,) + own.shape)
    return exchange(copies, axis, index_groups)


def split_parts(value):
    high = value.astype(jnp.bfloat16)
    low = (value - high.astype(jnp.float32)).astype(jnp.bfloat16)
    return high, low


def place(t, per_pair, n, strip):
    pair = t // per_pair
    return pair, n - 1 - pair, (t % per_pair) * strip


def add_up(terms):
    while len(terms) > 1:
        terms = [sum(terms[i + 1 : i + 2], terms[i]) for i in range(0, len(terms), 2)]
    return terms[0]


def invert_factor(block, spare):
    n_groups = BLOCK // 8
    lane = lax.broadcasted_iota(jnp.int32, (8, BLOCK), 1)
    sub = lax.broadcasted_iota(jnp.int32, (8, BLOCK), 0)
    rows = [block[8 * g : 8 * g + 8] for g in range(n_groups)]

    def pile(lines):
        result = lines[0]
        for a in range(1, 8):
            result = jnp.where(sub == a, lines[a], result)
        return result

    for begin in range(0, n_groups, SUB):
        end = begin + SUB
        lefts, rights = [], []
        for g in range(begin, end):
            k = 8 * g
            columns = [
                [jnp.broadcast_to(rows[h][:, k + a : k + a + 1], (8, BLOCK)) for h in range(g, end)]
                for a in range(8)
            ]
            inside = (lane >= k) & (lane < k + 8)
            slot = 72 * (g % 2)
            spare[slot : slot + 8, :] = rows[g]
            for a in range(8):
                spare[slot + 8 + 8 * a : slot + 16 + 8 * a, :] = columns[a][0]

            def spread(row):
                return jnp.broadcast_to(spare[slot + row : slot + row + 1, :], (8, BLOCK))

            line = [
                jnp.where(inside, jnp.where(lane == k + a, 1.0, 0.0), spread(a)) for a in range(8)
            ]
            held = {(a, b): spread(8 + 8 * b + a) for a in range(8) for b in range(a, 8)}
            columns = [column[1:] for column in columns]
            scaled, final = [], []
            for a in range(0, 8, 2):
                d = a + 1
                det = held[a, a] * held[d, d] - held[a, d] * held[a, d]
                inverse = 1.0 / held[a, a]
                inverse_d = held[a, a] * (1.0 / det)
                ratio = held[a, d] * inverse
                for c in range(d, 8):
                    held[d, c] = held[d, c] - ratio * held[a, c]
                line[d] = line[d] - ratio * line[a]
                columns[d] = [x - ratio * y for x, y in zip(columns[d], columns[a])]
                for b in range(d + 1, 8):
                    ratio, ratio_d = held[a, b] * inverse, held[d, b] * inverse_d
                    for c in range(b, 8):
                        held[b, c] = held[b, c] - ratio * held[a, c] - ratio_d * held[d, c]
                    line[b] = line[b] - ratio * line[a] - ratio_d * line[d]
                    columns[b] = [
                        x - ratio * y - ratio_d * z
                        for x, y, z in zip(columns[b], columns[a], columns[d])
                    ]
                scaled += [line[a] * inverse, line[d] * inverse_d]
                final += [line[a] * lax.rsqrt(held[a, a]), line[d] * lax.rsqrt(held[d, d])]
            for h in range(g + 1, end):
                taken = add_up([columns[a][h - g - 1] * scaled[a] for a in range(8)])
                rows[h] = jnp.where(inside, 0.0, rows[h]) - taken
            rows[g] = pile(final)
            lefts.append(jnp.where(lane >= 8 * end, rows[g], 0.0))
            rights.append(jnp.where((lane >= k + 8) & (lane < 8 * end), 0.0, rows[g]))
        if end < n_groups:
            taken = dot32(jnp.concatenate(lefts), jnp.concatenate(rights), 0)
            inside = (lane >= 8 * begin) & (lane < 8 * end)
            for h in range(end, n_groups):
                rows[h] = jnp.where(inside, 0.0, rows[h]) - taken[8 * h : 8 * h + 8]
    result = jnp.concatenate(rows, axis=0)
    r = lax.broadcasted_iota(jnp.int32, (BLOCK, BLOCK), 0)
    c = lax.broadcasted_iota(jnp.int32, (BLOCK, BLOCK), 1)
    return jnp.where(c <= r, result, 0.0)


def dot32(a, b, dim=1):
    return lax.dot_general(
        a, b, (((dim,), (0,)), ((), ())), precision=HI, preferred_element_type=jnp.float32
    )


def inverse_kernel(n, n_tp, core_ref, own_ref, other_ref, high_ref, low_ref, work, scale, corner, spare):
    per_pair = n_tp // (n // 2)
    strip = BLOCK // per_pair
    half = strip // 2
    core = core_ref[0]
    for t in range(n_tp):
        first, second, offset = place(t, per_pair, n, strip)
        width = (n - first) * BLOCK
        for source, c in ((own_ref, core), (other_ref, 1 - core)):
            for row, lanes in ((first, slice(0, width)), (second, slice(width, None))):
                start = pl.multiple_of(row * BLOCK + offset + c * half, half)
                work[pl.ds(start, half), row * BLOCK :] = source[t, :, lanes]

    r = lax.broadcasted_iota(jnp.int32, (BLOCK, BLOCK), 0)
    c = lax.broadcasted_iota(jnp.int32, (BLOCK, BLOCK), 1)
    tall = []
    for i in range(n):
        rows = slice(i * BLOCK, (i + 1) * BLOCK)
        diagonal = jnp.where(r == c, work[rows, rows], 0.0)
        scale[:, rows] = lax.rsqrt(jnp.sum(diagonal, axis=0, keepdims=True))
        tall.append(lax.rsqrt(jnp.sum(diagonal, axis=1, keepdims=True)))
    for i in range(n):
        rows, rest = slice(i * BLOCK, (i + 1) * BLOCK), slice(i * BLOCK, None)
        work[rows, rest] = work[rows, rest] * tall[i] * scale[:, rest]

    wide = 2 * BLOCK
    corner[:BLOCK, BLOCK:] = jnp.zeros((BLOCK, BLOCK), jnp.float32)

    @pl.loop(0, n // 2)
    def _(k):
        start = pl.multiple_of(k * wide, wide)
        here, top, bottom = pl.ds(start, wide), pl.ds(start, BLOCK), pl.ds(start + BLOCK, BLOCK)
        one = invert_factor(work[top, top], spare)
        cross = dot32(one, work[top, bottom])
        two = invert_factor(work[bottom, bottom] - dot32(cross, cross, 0), spare)
        corner[:BLOCK, :BLOCK] = one
        corner[BLOCK:, BLOCK:] = two
        corner[BLOCK:, :BLOCK] = -dot32(two, dot32(cross, one, 0))
        work[here, :] = dot32(corner[...], work[here, :])
        work[here, here] = corner[...]

        @pl.loop(k + 1, n // 2)
        def _(i):
            there = pl.ds(pl.multiple_of(i * wide, wide), wide)
            factor = work[here, there]
            work[there, here] = jnp.zeros((wide, wide), jnp.float32)
            work[there, :] -= dot32(factor, work[here, :], 0)

    for i in range(n // 2):
        rows = slice(i * wide, (i + 1) * wide)
        width = (i + 1) * wide
        high, low = split_parts(work[rows, :width] * scale[:, :width])
        high_ref[rows, :width] = high
        low_ref[rows, :width] = low
        if width < n * BLOCK:
            rest = jnp.zeros((wide, n * BLOCK - width), jnp.bfloat16)
            high_ref[rows, width:] = rest
            low_ref[rows, width:] = rest


def inverse_factor(core, own, other, rank):
    n_tp = own.shape[0]
    n = rank // BLOCK
    return pl.pallas_call(
        functools.partial(inverse_kernel, n, n_tp),
        out_shape=[jax.ShapeDtypeStruct((rank, rank), jnp.bfloat16)] * 2,
        in_specs=[pl.BlockSpec(memory_space=pltpu.SMEM)]
        + [pl.BlockSpec(memory_space=pltpu.VMEM)] * 2,
        out_specs=[pl.BlockSpec(memory_space=pltpu.VMEM)] * 2,
        scratch_shapes=[
            pltpu.VMEM((rank, rank), jnp.float32),
            pltpu.VMEM((1, rank), jnp.float32),
            pltpu.VMEM((2 * BLOCK, 2 * BLOCK), jnp.float32),
            pltpu.VMEM((144, BLOCK), jnp.float32),
        ],
        compiler_params=pltpu.CompilerParams(vmem_limit_bytes=40 * 1024 * 1024),
        cost_estimate=pl.CostEstimate(
            flops=12 * rank**3, bytes_accessed=8 * rank**2, transcendentals=0
        ),
    )(core, own, other)


def right_kernel(back_ref, high_ref, low_ref, right_ref, squares_ref):
    high, low = split_parts(back_ref[: right_ref.shape[0], :])
    wide = 2 * BLOCK
    for j in range(high_ref.shape[0] // wide):
        here, depth = slice(j * wide, (j + 1) * wide), slice(0, (j + 1) * wide)
        total = dot16(high[:, depth], high_ref[here, depth])
        total += dot16(high[:, depth], low_ref[here, depth])
        total += dot16(low[:, depth], high_ref[here, depth])
        right_ref[:, here] = total
        squares = jnp.sum(total * total, axis=0, keepdims=True)
        for t in range(squares_ref.shape[0]):
            squares_ref[t, :, here] = squares


def dot16(a, b):
    return lax.dot_general(a, b, (((1,), (1,)), ((), ())), preferred_element_type=jnp.float32)


def project(back, high, low, rows, n_tp):
    rank = back.shape[1]
    return pl.pallas_call(
        right_kernel,
        out_shape=[
            jax.ShapeDtypeStruct((rows, rank), jnp.float32),
            jax.ShapeDtypeStruct((n_tp, 1, rank), jnp.float32),
        ],
        in_specs=[pl.BlockSpec(memory_space=pltpu.VMEM)] * 3,
        out_specs=[pl.BlockSpec(memory_space=pltpu.VMEM)] * 2,
        compiler_params=pltpu.CompilerParams(vmem_limit_bytes=40 * 1024 * 1024),
        cost_estimate=pl.CostEstimate(
            flops=6 * rows * rank**2, bytes_accessed=8 * rank * rows, transcendentals=0
        ),
    )(back, high, low)


def per_device(momentum, grad, basis):
    n_fsdp, n_tp = lax.axis_size("fsdp"), lax.axis_size("tp")
    n_z = n_fsdp // 2
    z_groups, core_groups = groups(n_fsdp)
    rows, cols = momentum.shape
    share = basis.shape[1]
    rank = share * n_fsdp
    rows_all, cols_all = rows * n_fsdp, cols * n_tp
    me_fsdp, me_tp = lax.axis_index("fsdp"), lax.axis_index("tp")
    by_rows = (((0,), (0,)), ((), ()))
    by_cols = (((1,), (1,)), ((), ()))

    def dot(a, b, dims):
        return lax.dot_general(a, b, dims, preferred_element_type=jnp.float32)

    total = momentum.astype(jnp.float32) + grad.astype(jnp.float32)
    total_b = total.astype(jnp.bfloat16)
    basis_all = lax.all_gather(basis, "fsdp", axis=1, tiled=True)
    part = jnp.dot(total_b, basis_all, preferred_element_type=jnp.float32).astype(jnp.bfloat16)
    arrived = exchange(part.reshape(n_tp, rows // n_tp, rank), "tp")
    left_own = jnp.sum(arrived.astype(jnp.float32), axis=0).astype(jnp.bfloat16)
    left = collect(left_own, "tp", n_tp).reshape(rows, rank)

    n = rank // BLOCK
    per_pair = n_tp // (n // 2)
    strip = BLOCK // per_pair
    pair, mirror, offset = place(me_tp, per_pair, n, strip)
    made = []
    for row in (pair, mirror):
        mine = lax.dynamic_slice_in_dim(left, row * BLOCK + offset, strip, 1)
        made.append(dot(mine, left, by_rows))
    packed = lax.select_n(
        pair,
        *[
            jnp.concatenate([made[0][:, p * BLOCK :], made[1][:, (n - 1 - p) * BLOCK :]], axis=1)
            for p in range(n // 2)
        ],
    )
    packed = packed.reshape(2, strip // 2, packed.shape[1])
    packed = jnp.sum(exchange(packed, "fsdp", core_groups), axis=0)
    packed = jnp.sum(collect(packed, "fsdp", n_z, z_groups), axis=0)
    own = collect(packed, "tp", n_tp)
    other = lax.ppermute(own, "fsdp", [(i, i ^ 1) for i in range(n_fsdp)])

    back = dot(total_b, left, by_rows)
    padded = -(-cols // (8 * n_fsdp)) * 8 * n_fsdp
    back = jnp.pad(back, ((0, padded - cols), (0, 0)))
    back = lax.psum_scatter(back, "fsdp", scatter_dimension=0, tiled=True)
    back = lax.all_gather(back, "fsdp", axis=0, tiled=True)

    core = (me_fsdp % 2).astype(jnp.int32).reshape(1)
    inverse_high, inverse_low = inverse_factor(core, own, other, rank)
    right, squares = project(back, inverse_high, inverse_low, cols, n_tp)
    left, squares = lax.optimization_barrier((left, squares))
    squares = exchange(squares, "tp")
    ortho = dot(left, inverse_high, by_cols) + dot(left, inverse_low, by_cols)
    ortho_b = ortho.astype(jnp.bfloat16)
    scale = jnp.sqrt(jnp.sum(squares, axis=(0, 1)) / cols_all + epsilon)
    right_b = right.astype(jnp.bfloat16)
    basis_full = (right / scale[None, :]).astype(jnp.bfloat16)
    basis_new = lax.dynamic_slice_in_dim(basis_full, me_fsdp * share, share, 1)
    correction = dot(ortho_b, right_b, by_cols)
    raw = dot(ortho_b, basis_full, by_cols)
    momentum_new = (total - (1.0 - keep_rate) * correction).astype(jnp.bfloat16)
    update = (math.sqrt(rows_all / rank) * raw).astype(jnp.bfloat16)
    return (momentum_new, basis_new, update)


def solution(mesh):
    return jax.shard_map(
        per_device,
        mesh=mesh,
        in_specs=(P("fsdp", "tp"), P("fsdp", "tp"), P("tp", "fsdp")),
        out_specs=(P("fsdp", "tp"), P("tp", "fsdp"), P("fsdp", "tp")),
        check_vma=False,
    )
```

time: 656 us -> 253 us (0.39); the launches traced: 647 us -> 253 us
  other arithmetic: 272 us -> 0.54 us
  waiting for transfers between devices: 107 us -> 38 us
  matrix products: 57.9 us -> 12.3 us
  Pallas kernels: 0 us -> 39 us
  local copies, waits for them, and re-layouts: 49.5 us -> 11.2 us
  starting transfers between devices: 26.6 us -> 19 us
    another operation x35 -> x0, other arithmetic: 263 us -> none  [the longest x30 174 us: per_device(): chol = jnp.linalg.cholesky(gram)]
    all_to_all x3 -> x2, waiting for transfers between devices: 98.9 us -> 6.67 us  [exchange(): lax.all_to_all(pieces, axis, 0, 0, tiled=True, axis_index_groups=index_gr...]
    another operation x29 -> x0, matrix products: 46.7 us -> none  [the longest x15 23.6 us: per_device(): lax.linalg.triangular_solve(chol, jnp.concatenate([left, back]), left_sid...]
    pallas_call x0 -> x2, Pallas kernels: none -> 39 us  [the longest x1 36.4 us: inverse_factor(): pl.pallas_call(functools.partial(inverse_kernel, n, n_tp), out_shape=[jax...]
    another operation x33 -> x0, local copies, waits for them, and re-layouts: 31.2 us -> none
    reduce_scatter x1, waiting for transfers between devices: 7.98 us -> 29 us  [per_device(): back = lax.psum_scatter(back, 'fsdp', scatter_dimension=0, tiled=True)]
    all_to_all x3 -> x2, starting transfers between devices: 21.9 us -> 14 us  [exchange(): lax.all_to_all(pieces, axis, 0, 0, tiled=True, axis_index_groups=index_gr...]
    all_to_all x3 -> x4, blocking collectives: 86.4 us -> 90.8 us  [exchange(): lax.all_to_all(pieces, axis, 0, 0, tiled=True, axis_index_groups=index_gr...]
  transfers between devices with their start and end apart: 6 -> 5, of which waited for: 4 -> 3; matrix products, arithmetic and copies ran while one was open for 52% -> 2% of each run, Pallas kernels for 0% -> 14%
where the time goes in v2:
time: 253 us
  blocking collectives  118 us (47%)
  Pallas kernels  39 us (15%)
  waiting for transfers between devices  38 us (15%)
  starting transfers between devices  19 us (8%)
  between operations  14.2 us (6%)
  matrix products  12.3 us (5%)
  local copies, waits for them, and re-layouts  11.2 us (4%)
    all_to_all x4, blocking collectives, exchange(): lax.all_to_all(pieces, axis, 0, 0, tiled=True, axis_index_groups=index_gr...  90.8 us
    pallas_call x1, Pallas kernels, inverse_factor(): pl.pallas_call(functools.partial(inverse_kernel, n, n_tp), out_shape=[jax...  36.4 us
    reduce_scatter x1, waiting for transfers between devices, per_device(): back = lax.psum_scatter(back, 'fsdp', scatter_dimension=0, tiled=True)  29 us
    all_gather x1, blocking collectives, per_device(): basis_all = lax.all_gather(basis, 'fsdp', axis=1, tiled=True)  27.7 us
    all_to_all x2, starting transfers between devices, exchange(): lax.all_to_all(pieces, axis, 0, 0, tiled=True, axis_index_groups=index_gr...  14 us
    dot_general x7, matrix products, dot(): return lax.dot_general(a, b, dims, preferred_element_type=jnp.float32)  10.4 us
    unnamed x17, local copies, waits for them, and re-layouts  8.13 us
    all_to_all x2, waiting for transfers between devices, exchange(): lax.all_to_all(pieces, axis, 0, 0, tiled=True, axis_index_groups=index_gr...  6.67 us
  transfers between devices with their start and end apart: 5, of which 3 were waited for; matrix products, arithmetic and copies ran while one was open for 2% of the time, Pallas kernels for 14%

profile of v2, /device:TPU:1, one launch (start us, length us, event | category | flops | bytes accessed | tf_op | source)
XLA Modules:
  0.0 252.8 jit_solution(5646610520563108910)
XLA Ops:
  7.2 0.0 reduce-scatter.2.cloned.1.call-start
  7.2 27.7 %all_gather.6 = bf16[448,1024]{0,1:T(8,128)(2,1)S(1)} all-gather(bf16[448,64]{0,1:T(8,128)(2,1)} %param.5), channel_id=1, replica_groups=mesh['fsdp'=16,'tp'=32] {'fsdp'}, dimensions={1}, use_global_device_ids=true | all-gather | bytes 974848 | tf_op jit(solution)/shard_map/all_gather | solution.py:264
  34.9 1.9 convolution_convert_fusion
  36.9 36.6 %all_to_all.30 = bf16[32,16,1024]{2,1,0:T(8,128)(2,1)S(1)} all-to-all(bf16[32,16,1024]{2,1,0:T(8,128)(2,1)S(1)} %bitcast.35), channel_id=1, replica_groups=mesh['fsdp'=16,'tp'=32] {'tp'}, dimensions={0} | all-to-all | bytes 2097152 | tf_op jit(solution)/shard_map/all_to_all | solution.py:25
  73.4 0.0 copy-start.5
  73.4 0.0 copy-start.7
  73.4 0.2 reduce_sum.39
  73.6 0.1 broadcast_in_dim.6
  73.7 31.3 %all_to_all.31 = bf16[32,16,1024]{2,1,0:T(8,128)(2,1)S(1)} all-to-all(bf16[32,16,1024]{2,1,0:T(8,128)(2,1)S(1)} %broadcast_in_dim.6), channel_id=1, replica_groups=mesh['fsdp'=16,'tp'=32] {'tp'}, dimensions={0} | all-to-all | bytes 2097152 | tf_op jit(solution)/shard_map/all_to_all | solution.py:25
  105.0 0.0 copy-done.5
  105.0 0.0 copy-done.7
  105.0 0.6 fusion.5
  105.7 1.7 pad.4
  107.4 0.0 reduce-scatter.2.cloned.1.call-update
  107.4 0.4 fusion.8
  107.8 0.4 fusion.10
  108.3 6.8 %all_to_all.32 = f32[2,8,1152]{2,1,0:T(8,128)S(1)} all-to-all(f32[2,8,1152]{2,1,0:T(8,128)S(1)} %fusion.12), channel_id=1, replica_groups={{0,32},{64,96},{128,160},{192,224},{256,288},{320,352},{384,416},{448,4..., dimensions={0} | all-to-all | bytes 147456 | tf_op jit(solution)/shard_map/all_to_all | solution.py:25
  115.1 16.1 %all_to_all.33 = f32[8,8,1152]{2,1,0:T(8,128)S(1)} all-to-all(f32[8,8,1152]{2,1,0:T(8,128)S(1)} %broadcast_in_dim.7), channel_id=1, replica_groups={{0,64,128,192,256,320,384,448},{32,96,160,224,288,352,416,480},{1,65,12..., dimensions={0} | all-to-all | bytes 589824 | tf_op jit(solution)/shard_map/all_to_all | solution.py:25
  131.2 1.1 broadcast_in_dim.8
  132.3 5.0 %all-to-all-start.4 = ((f32[32,8,1152]{2,1,0:T(8,128)}), f32[32,8,1152]{2,1,0:T(8,128)S(1)}, u32[]{:S(2)}, u32[]{:S(2)}) async-start(f32[32,8,1152]{2,1,0:T(8,128)} %broadcast_in_dim.8), calls=%async_computation.5 | async-start | bytes 2359296 | tf_op jit(solution)/shard_map/all_to_all | solution.py:25
  137.3 0.0 all-gather.2.cloned.1.call-start
  137.4 29.0 %reduce-scatter.2.cloned.1.call-done = f32[32,1024]{1,0:T(8,128)} async-done(((f32[512,1024]{1,0:T(8,128)}), f32[32,1024]{1,0:T(8,128)}) %reduce-scatter.2.cloned.1.call-update) | async-done | bytes 131088 | tf_op jit(solution)/shard_map/reduce_scatter | solution.py:294
  166.4 0.0 all-gather.2.cloned.1.call-update
  166.4 0.0 all-to-all-done.4.own_ref
  166.4 4.9 %collective-permute-start = (f32[32,8,1152]{2,1,0:T(8,128)S(1)}, f32[32,8,1152]{2,1,0:T(8,128)S(1)}, u32[]{:S(2)}, u32[]{:S(2)}) collective-permute-start(f32[32,8,1152]{2,1,0:T(8,128)S(1)} %all-to-all-done.4.own_ref), channel_id=1, source_target_pairs={{0,32},{32,0},{64,96},{96,64},{128,160},{160,128},{192,224},{224,1... | collective-permute-start | bytes 3538952 | tf_op jit(solution)/shard_map/ppermute | solution.py:289
  171.3 2.3 collective-permute-done.other_ref
  173.6 36.4 %shard_map.58 = (bf16[1024,1024]{1,0:T(8,128)(2,1)S(1)}, bf16[1024,1024]{1,0:T(8,128)(2,1)S(1)}) custom-call(s32[1]{0:T(128)} %bitcast.2.core_ref, f32[32,8,1152]{2,1,0:T(8,128)S(1)} %all-to-all-done.4.own_ref, f32[32,8,1152]{2,1,0:T(8,128)S(1)} %collective-permute-done.other_ref), custom_call_target="tpu_custom_call" | custom-call | flops 12884901888 | bytes 8388608 | tf_op jit(solution)/shard_map/pallas_call | solution.py:193
  210.0 0.0 copy-start.1
  210.0 1.3 copy-done.1
  211.3 0.0 copy-start.3
  211.3 1.3 copy-done.3
  212.6 0.0 all-gather.2.cloned.1.call-done.back_ref
  212.6 1.6 copy-done
  214.2 1.6 copy-done.2
  215.8 1.6 copy-done.4
  217.4 2.7 %shard_map.59 = (f32[448,1024]{1,0:T(8,128)S(1)}, f32[32,1,1024]{2,1,0:T(1,128)}) custom-call(f32[512,1024]{1,0:T(8,128)S(1)} %copy-done, bf16[1024,1024]{1,0:T(8,128)(2,1)S(1)} %copy-done.2, bf16[1024,1024]{1,0:T(8,128)(2,1)S(1)} %copy-done.4), custom_call_target="tpu_custom_call" | custom-call | flops 2818572288 | bytes 3670016 | tf_op jit(solution)/shard_map/pallas_call | solution.py:232
  220.1 1.3 fusion.15
  221.4 0.0 copy-start.6
  221.4 2.3 add_convert_fusion
  223.6 9.0 %all-to-all-start.5 = ((f32[32,1,1024]{2,1,0:T(1,128)}), f32[32,1,1024]{2,1,0:T(1,128)S(1)}, u32[]{:S(2)}, u32[]{:S(2)}) async-start(f32[32,1,1024]{2,1,0:T(1,128)} %get-tuple-element.14), calls=%async_computation.6 | async-start | bytes 262144 | tf_op jit(solution)/shard_map/all_to_all | solution.py:25
  232.7 0.0 copy-done.6
  232.7 2.8 %fusion.2 = bf16[512,448]{0,1:T(8,128)(2,1)} fusion(bf16[512,1024]{1,0:T(8,128)(2,1)} %add_convert_fusion, f32[448,1024]{1,0:T(8,128)S(1)} %get-tuple-element.13, bf16[512,448]{0,1:T(8,128)(2,1)S(1)} %copy-done.6, bf16[512,448]{0,1:T(8,128)(2,1)} %param.3), kind=kOutput, calls=%fused_computation.7 | convolution fusion | flops 471597056 | bytes 4259840 | tf_op jit(solution)/shard_map/dot_general | solution.py:260
  235.4 6.7 %all-to-all-done.5 = f32[32,1,1024]{2,1,0:T(1,128)S(1)} async-done(((f32[32,1,1024]{2,1,0:T(1,128)}), f32[32,1,1024]{2,1,0:T(1,128)S(1)}, u32[]{:S(2)}, u32[]{:S(2)}) %all-to-all-start.5) | async-done | bytes 131104 | tf_op jit(solution)/shard_map/all_to_all | solution.py:25
  242.1 0.1 reduce_sum.42
  242.2 0.2 divide_convert_fusion
  242.5 2.7 %fusion.1 = bf16[512,448]{0,1:T(8,128)(2,1)} fusion(bf16[512,1024]{1,0:T(8,128)(2,1)} %add_convert_fusion, bf16[448,1024]{1,0:T(8,128)(2,1)S(1)} %divide_convert_fusion), kind=kOutput, calls=%fused_computation.6 | convolution fusion | flops 470220800 | bytes 2424832 | tf_op jit(solution)/shard_map/dot_general | solution.py:260
  245.1 0.1 constant_dynamic-slice_fusion
  245.2 0.7 copy.7
  (15 shorter events, 0.1 us)
Async XLA Ops:
  7.2 159.2 %reduce-scatter.2.cloned.1.call-start = ((), (), s32[]{:S(2)}) async-start(), calls=%async_computation.7 | async-start | bytes 2228224 | tf_op jit(solution)/shard_map/reduce_scatter | solution.py:294
  73.4 31.6 %copy-start.5 = (bf16[512,448]{0,1:T(8,128)(2,1)S(1)}, bf16[512,448]{0,1:T(8,128)(2,1)}, u32[]{:S(2)}) copy-start(bf16[512,448]{0,1:T(8,128)(2,1)} %param.4) | copy-start | bytes 1376260
  73.4 31.6 %copy-start.7 = (bf16[512,448]{0,1:T(8,128)(2,1)S(1)}, bf16[512,448]{0,1:T(8,128)(2,1)}, u32[]{:S(2)}) copy-start(bf16[512,448]{0,1:T(8,128)(2,1)} %param.3) | copy-start | bytes 1376260
  132.3 34.1 %all-to-all-start.4 = ((f32[32,8,1152]{2,1,0:T(8,128)}), f32[32,8,1152]{2,1,0:T(8,128)S(1)}, u32[]{:S(2)}, u32[]{:S(2)}) async-start(f32[32,8,1152]{2,1,0:T(8,128)} %broadcast_in_dim.8), calls=%async_computation.5 | async-start | bytes 2359296 | tf_op jit(solution)/shard_map/all_to_all | solution.py:25
  137.3 75.3 %all-gather.2.cloned.1.call-start = ((), (), s32[]{:S(2)}) async-start(), calls=%async_computation.8 | async-start | bytes 2228224 | tf_op jit(solution)/shard_map/all_gather | solution.py:295
  166.4 7.2 %collective-permute-start = (f32[32,8,1152]{2,1,0:T(8,128)S(1)}, f32[32,8,1152]{2,1,0:T(8,128)S(1)}, u32[]{:S(2)}, u32[]{:S(2)}) collective-permute-start(f32[32,8,1152]{2,1,0:T(8,128)S(1)} %all-to-all-done.4.own_ref), channel_id=1, source_target_pairs={{0,32},{32,0},{64,96},{96,64},{128,160},{160,128},{192,224},{224,1... | collective-permute-start | bytes 3538952 | tf_op jit(solution)/shard_map/ppermute | solution.py:289
  210.0 1.3 copy-start.1
  211.3 1.3 copy-start.3
  212.6 1.6 copy-start
  214.2 1.6 copy-start.2
  215.8 1.6 copy-start.4
  221.4 11.3 %copy-start.6 = (bf16[512,448]{0,1:T(8,128)(2,1)S(1)}, bf16[512,448]{0,1:T(8,128)(2,1)}, u32[]{:S(2)}) copy-start(bf16[512,448]{0,1:T(8,128)(2,1)} %param.4) | copy-start | bytes 1376260
  223.6 18.5 %all-to-all-start.5 = ((f32[32,1,1024]{2,1,0:T(1,128)}), f32[32,1,1024]{2,1,0:T(1,128)S(1)}, u32[]{:S(2)}, u32[]{:S(2)}) async-start(f32[32,1,1024]{2,1,0:T(1,128)} %get-tuple-element.14), calls=%async_computation.6 | async-start | bytes 262144 | tf_op jit(solution)/shard_map/all_to_all | solution.py:25
Sparse Core Ops, SparseCore 0:
  107.5 58.8 reduce-scatter.1
  168.5 43.8 all-gather.1

commit v3 on v2

--- a/solution.py
+++ b/solution.py
@@ -47,7 +47,7 @@
     return terms[0]
 
 
-def invert_factor(block, spare):
+def invert_factor(block, spare, aside):
     n_groups = BLOCK // 8
     lane = lax.broadcasted_iota(jnp.int32, (8, BLOCK), 1)
     sub = lax.broadcasted_iota(jnp.int32, (8, BLOCK), 0)
@@ -108,6 +108,8 @@
                 taken = add_up([columns[a][h - g - 1] * scaled[a] for a in range(8)])
                 rows[h] = jnp.where(inside, 0.0, rows[h]) - taken
             rows[g] = pile(final)
+            if aside:
+                aside.pop(0)()
             lefts.append(jnp.where(lane >= 8 * end, rows[g], 0.0))
             rights.append(jnp.where((lane >= k + 8) & (lane < 8 * end), 0.0, rows[g]))
         if end < n_groups:
@@ -127,7 +129,10 @@
     )
 
 
-def inverse_kernel(n, n_tp, core_ref, own_ref, other_ref, high_ref, low_ref, work, scale, corner, spare):
+def inverse_kernel(
+    n, n_tp, core_ref, own_ref, other_ref, high_out, low_out,
+    work, scale, corners, spare, high_ref, low_ref, sems,
+):
     per_pair = n_tp // (n // 2)
     strip = BLOCK // per_pair
     half = strip // 2
@@ -153,38 +158,68 @@
         work[rows, rest] = work[rows, rest] * tall[i] * scale[:, rest]
 
     wide = 2 * BLOCK
-    corner[:BLOCK, BLOCK:] = jnp.zeros((BLOCK, BLOCK), jnp.float32)
-
-    @pl.loop(0, n // 2)
-    def _(k):
-        start = pl.multiple_of(k * wide, wide)
-        here, top, bottom = pl.ds(start, wide), pl.ds(start, BLOCK), pl.ds(start + BLOCK, BLOCK)
-        one = invert_factor(work[top, top], spare)
+    n_wide = n // 2
+    spans = [slice(i * wide, (i + 1) * wide) for i in range(n_wide)]
+
+    def advance(k, j):
+        work[spans[k], spans[j]] = dot32(corners[k % 2], work[spans[k], spans[j]])
+
+    def take(k, i, j):
+        change = dot32(work[spans[k], spans[i]], work[spans[k], spans[j]], 0)
+        if j == k:
+            work[spans[i], spans[j]] = -change
+        else:
+            work[spans[i], spans[j]] -= change
+
+    def copies(k):
+        return [
+            pltpu.make_async_copy(part.at[spans[k]], out.at[spans[k]], sems.at[p, k])
+            for p, (part, out) in enumerate(((high_ref, high_out), (low_ref, low_out)))
+        ]
+
+    def finish(k):
+        width = (k + 1) * wide
+        high, low = split_parts(work[spans[k], :width] * scale[:, :width])
+        high_ref[spans[k], :width] = high
+        low_ref[spans[k], :width] = low
+        if k + 1 < n_wide:
+            rest = jnp.zeros((wide, n * BLOCK - width), jnp.bfloat16)
+            high_ref[spans[k], width:] = rest
+            low_ref[spans[k], width:] = rest
+        for copy in copies(k):
+            copy.start()
+
+    aside = []
+    for k in range(n_wide):
+        here, corner = spans[k], corners.at[k % 2]
+        top, bottom = slice(k * wide, k * wide + BLOCK), slice(k * wide + BLOCK, (k + 1) * wide)
+        one = invert_factor(work[top, top], spare, aside)
         cross = dot32(one, work[top, bottom])
-        two = invert_factor(work[bottom, bottom] - dot32(cross, cross, 0), spare)
+        two = invert_factor(work[bottom, bottom] - dot32(cross, cross, 0), spare, aside)
+        while aside:
+            aside.pop(0)()
         corner[:BLOCK, :BLOCK] = one
+        corner[:BLOCK, BLOCK:] = jnp.zeros((BLOCK, BLOCK), jnp.float32)
         corner[BLOCK:, BLOCK:] = two
         corner[BLOCK:, :BLOCK] = -dot32(two, dot32(cross, one, 0))
-        work[here, :] = dot32(corner[...], work[here, :])
         work[here, here] = corner[...]
-
-        @pl.loop(k + 1, n // 2)
-        def _(i):
-            there = pl.ds(pl.multiple_of(i * wide, wide), wide)
-            factor = work[here, there]
-            work[there, here] = jnp.zeros((wide, wide), jnp.float32)
-            work[there, :] -= dot32(factor, work[here, :], 0)
-
-    for i in range(n // 2):
-        rows = slice(i * wide, (i + 1) * wide)
-        width = (i + 1) * wide
-        high, low = split_parts(work[rows, :width] * scale[:, :width])
-        high_ref[rows, :width] = high
-        low_ref[rows, :width] = low
-        if width < n * BLOCK:
-            rest = jnp.zeros((wide, n * BLOCK - width), jnp.bfloat16)
-            high_ref[rows, width:] = rest
-            low_ref[rows, width:] = rest
+        if k + 1 < n_wide:
+            advance(k, k + 1)
+            take(k, k + 1, k + 1)
+        others = [j for j in range(n_wide) if j not in (k, k + 1)]
+        aside += [functools.partial(advance, k, j) for j in others]
+        aside += [
+            functools.partial(take, k, i, j)
+            for i in range(k + 1, n_wide)
+            for j in range(n_wide)
+            if (j <= k or j >= i) and (i, j) != (k + 1, k + 1)
+        ]
+        aside.append(functools.partial(finish, k))
+    while aside:
+        aside.pop(0)()
+    for k in range(n_wide):
+        for copy in copies(k):
+            copy.wait()
 
 
 def inverse_factor(core, own, other, rank):
@@ -195,59 +230,99 @@
         out_shape=[jax.ShapeDtypeStruct((rank, rank), jnp.bfloat16)] * 2,
         in_specs=[pl.BlockSpec(memory_space=pltpu.SMEM)]
         + [pl.BlockSpec(memory_space=pltpu.VMEM)] * 2,
-        out_specs=[pl.BlockSpec(memory_space=pltpu.VMEM)] * 2,
+        out_specs=[pl.BlockSpec(memory_space=pl.ANY)] * 2,
         scratch_shapes=[
             pltpu.VMEM((rank, rank), jnp.float32),
             pltpu.VMEM((1, rank), jnp.float32),
-            pltpu.VMEM((2 * BLOCK, 2 * BLOCK), jnp.float32),
+            pltpu.VMEM((2, 2 * BLOCK, 2 * BLOCK), jnp.float32),
             pltpu.VMEM((144, BLOCK), jnp.float32),
+            pltpu.VMEM((rank, rank), jnp.bfloat16),
+            pltpu.VMEM((rank, rank), jnp.bfloat16),
+            pltpu.SemaphoreType.DMA((2, n // 2)),
         ],
-        compiler_params=pltpu.CompilerParams(vmem_limit_bytes=40 * 1024 * 1024),
+        compiler_params=pltpu.CompilerParams(vmem_limit_bytes=32 * 1024 * 1024),
         cost_estimate=pl.CostEstimate(
             flops=12 * rank**3, bytes_accessed=8 * rank**2, transcendentals=0
         ),
     )(core, own, other)
 
 
-def right_kernel(back_ref, high_ref, low_ref, right_ref, squares_ref):
-    high, low = split_parts(back_ref[: right_ref.shape[0], :])
-    wide = 2 * BLOCK
-    for j in range(high_ref.shape[0] // wide):
-        here, depth = slice(j * wide, (j + 1) * wide), slice(0, (j + 1) * wide)
-        total = dot16(high[:, depth], high_ref[here, depth])
-        total += dot16(high[:, depth], low_ref[here, depth])
-        total += dot16(low[:, depth], high_ref[here, depth])
-        right_ref[:, here] = total
-        squares = jnp.sum(total * total, axis=0, keepdims=True)
-        for t in range(squares_ref.shape[0]):
-            squares_ref[t, :, here] = squares
-
-
 def dot16(a, b):
     return lax.dot_general(a, b, (((1,), (1,)), ((), ())), preferred_element_type=jnp.float32)
 
 
-def project(back, high, low, rows, n_tp):
+def right_kernel(chunk, back_ref, high_ref, low_ref, right_ref, squares_ref, back_high, back_low):
+    rows = right_ref.shape[0]
+
+    @pl.when(pl.program_id(0) == 0)
+    def _():
+        for start in range(0, rows, chunk):
+            core, z = divmod(start, rows // 2)
+            source = (2 * (z // chunk) + core) * chunk
+            high, low = split_parts(back_ref[source : source + chunk, :])
+            back_high[start : start + chunk, :] = high
+            back_low[start : start + chunk, :] = low
+
+    total = dot16(back_high[...], high_ref[...])
+    total += dot16(back_high[...], low_ref[...])
+    total += dot16(back_low[...], high_ref[...])
+    right_ref[...] = total
+    squares = jnp.sum(total * total, axis=0, keepdims=True)
+    for t in range(squares_ref.shape[0]):
+        squares_ref[t] = squares
+
+
+def project(back, high, low, rows, chunk, n_tp):
     rank = back.shape[1]
+    wide = 2 * BLOCK
+    whole = pl.BlockSpec(back.shape, lambda j: (0, 0))
+    block = pl.BlockSpec((wide, rank), lambda j: (j, 0))
     return pl.pallas_call(
-        right_kernel,
+        functools.partial(right_kernel, chunk),
         out_shape=[
             jax.ShapeDtypeStruct((rows, rank), jnp.float32),
             jax.ShapeDtypeStruct((n_tp, 1, rank), jnp.float32),
         ],
-        in_specs=[pl.BlockSpec(memory_space=pltpu.VMEM)] * 3,
-        out_specs=[pl.BlockSpec(memory_space=pltpu.VMEM)] * 2,
-        compiler_params=pltpu.CompilerParams(vmem_limit_bytes=40 * 1024 * 1024),
+        grid=(rank // wide,),
+        in_specs=[whole, block, block],
+        out_specs=[
+            pl.BlockSpec((rows, wide), lambda j: (0, j)),
+            pl.BlockSpec((n_tp, 1, wide), lambda j: (0, 0, j)),
+        ],
+        scratch_shapes=[pltpu.VMEM((rows, rank), jnp.bfloat16)] * 2,
+        compiler_params=pltpu.CompilerParams(vmem_limit_bytes=24 * 1024 * 1024),
         cost_estimate=pl.CostEstimate(
             flops=6 * rows * rank**2, bytes_accessed=8 * rank * rows, transcendentals=0
         ),
     )(back, high, low)
 
 
+def ortho_kernel(left_ref, high_ref, low_ref, ortho_ref):
+    total = dot16(left_ref[...], high_ref[...])
+    total += dot16(left_ref[...], low_ref[...])
+    ortho_ref[...] = total.astype(jnp.bfloat16)
+
+
+def orthonormal(left, high, low):
+    rows, rank = left.shape
+    wide = 2 * BLOCK
+    block = pl.BlockSpec((wide, rank), lambda j: (j, 0))
+    return pl.pallas_call(
+        ortho_kernel,
+        out_shape=jax.ShapeDtypeStruct((rows, rank), jnp.bfloat16),
+        grid=(rank // wide,),
+        in_specs=[pl.BlockSpec(left.shape, lambda j: (0, 0)), block, block],
+        out_specs=pl.BlockSpec((rows, wide), lambda j: (0, j)),
+        compiler_params=pltpu.CompilerParams(vmem_limit_bytes=24 * 1024 * 1024),
+        cost_estimate=pl.CostEstimate(flops=0, bytes_accessed=0, transcendentals=0),
+    )(left, high, low)
+
+
 def per_device(momentum, grad, basis):
     n_fsdp, n_tp = lax.axis_size("fsdp"), lax.axis_size("tp")
     n_z = n_fsdp // 2
     z_groups, core_groups = groups(n_fsdp)
+    swap = [(i, i ^ 1) for i in range(n_fsdp)]
     rows, cols = momentum.shape
     share = basis.shape[1]
     rank = share * n_fsdp
@@ -286,21 +361,28 @@
     packed = jnp.sum(exchange(packed, "fsdp", core_groups), axis=0)
     packed = jnp.sum(collect(packed, "fsdp", n_z, z_groups), axis=0)
     own = collect(packed, "tp", n_tp)
-    other = lax.ppermute(own, "fsdp", [(i, i ^ 1) for i in range(n_fsdp)])
-
-    back = dot(total_b, left, by_rows)
-    padded = -(-cols // (8 * n_fsdp)) * 8 * n_fsdp
-    back = jnp.pad(back, ((0, padded - cols), (0, 0)))
-    back = lax.psum_scatter(back, "fsdp", scatter_dimension=0, tiled=True)
-    back = lax.all_gather(back, "fsdp", axis=0, tiled=True)
-
-    core = (me_fsdp % 2).astype(jnp.int32).reshape(1)
-    inverse_high, inverse_low = inverse_factor(core, own, other, rank)
-    right, squares = project(back, inverse_high, inverse_low, cols, n_tp)
+    other = lax.ppermute(own, "fsdp", swap)
+
+    core = me_fsdp % 2
+    half = cols // 2
+    chunk = -(-half // (32 * n_z)) * 32
+    spread = jnp.pad(total_b.reshape(rows, 2, half), ((0, 0), (0, 0), (0, chunk * n_z - half)))
+    back = dot(spread.reshape(rows, 2 * chunk * n_z), left, by_rows)
+    back = back.reshape(2, chunk * n_z, rank)
+    theirs = lax.dynamic_index_in_dim(back, 1 - core, 0, False)
+    mine = lax.dynamic_index_in_dim(back, core, 0, False)
+    mine = mine + lax.ppermute(theirs, "fsdp", swap)
+    mine = lax.psum_scatter(
+        mine, "fsdp", scatter_dimension=0, tiled=True, axis_index_groups=z_groups
+    )
+    back = lax.all_gather(mine, "fsdp", axis=0, tiled=True)
+
+    parity = core.astype(jnp.int32).reshape(1)
+    inverse_high, inverse_low = inverse_factor(parity, own, other, rank)
+    right, squares = project(back, inverse_high, inverse_low, cols, chunk, n_tp)
     left, squares = lax.optimization_barrier((left, squares))
     squares = exchange(squares, "tp")
-    ortho = dot(left, inverse_high, by_cols) + dot(left, inverse_low, by_cols)
-    ortho_b = ortho.astype(jnp.bfloat16)
+    ortho_b = orthonormal(left, inverse_high, inverse_low)
     scale = jnp.sqrt(jnp.sum(squares, axis=(0, 1)) / cols_all + epsilon)
     right_b = right.astype(jnp.bfloat16)
     basis_full = (right / scale[None, :]).astype(jnp.bfloat16)

time: 253 us -> 249 us (0.984)
  blocking collectives: 118 us -> 85.9 us
  waiting for transfers between devices: 38 us -> 58.3 us
  starting transfers between devices: 19 us -> 26.6 us
  matrix products: 12.3 us -> 5.1 us
  local copies, waits for them, and re-layouts: 11.2 us -> 15 us
    all_to_all x2 -> x3, waiting for transfers between devices: 6.67 us -> 47.3 us  [exchange(): lax.all_to_all(pieces, axis, 0, 0, tiled=True, axis_index_groups=index_gr...]
    all_to_all x4 -> x3, blocking collectives: 90.8 us -> 58.2 us  [exchange(): lax.all_to_all(pieces, axis, 0, 0, tiled=True, axis_index_groups=index_gr...]
    reduce_scatter x1, waiting for transfers between devices: 29 us -> 7.14 us  [per_device(): lax.psum_scatter(mine, 'fsdp', scatter_dimension=0, tiled=True, axis_inde...]
    dot_general x7 -> x5, matrix products: 10.4 us -> 4.33 us  [dot(): return lax.dot_general(a, b, dims, preferred_element_type=jnp.float32)]
    ppermute x1 -> x2, starting transfers between devices: 4.92 us -> 10.7 us  [the longest x1 5.46 us: per_device(): other = lax.ppermute(own, 'fsdp', swap)]
    pallas_call x1 -> x2, Pallas kernels: 2.67 us -> 7.77 us  [the longest x1 4.69 us: project(): pl.pallas_call(functools.partial(right_kernel, chunk), out_shape=[jax.Sha...]
    unnamed x17 -> x23, local copies, waits for them, and re-layouts: 8.13 us -> 12.5 us
    pallas_call x1, Pallas kernels: 36.4 us -> 32.3 us  [inverse_factor(): pl.pallas_call(functools.partial(inverse_kernel, n, n_tp), out_shape=[jax...]
  transfers between devices with their start and end apart: 5 -> 7, of which waited for: 3 -> 6; matrix products, arithmetic and copies ran while one was open for 2% -> 1% of each run, Pallas kernels for 14% -> 14%
where the time goes in v3:
time: 249 us; the launch traced here: 248 us
  blocking collectives  85.9 us (34%)
  waiting for transfers between devices  58.3 us (23%)
  Pallas kernels  40.1 us (16%)
  starting transfers between devices  26.6 us (11%)
  local copies, waits for them, and re-layouts  15 us (6%)
  between operations  14.3 us (6%)
  matrix products  5.1 us (2%)
  other arithmetic  2.93 us (1%)
    all_to_all x3, blocking collectives, exchange(): lax.all_to_all(pieces, axis, 0, 0, tiled=True, axis_index_groups=index_gr...  58.2 us
    all_to_all x3, waiting for transfers between devices, exchange(): lax.all_to_all(pieces, axis, 0, 0, tiled=True, axis_index_groups=index_gr...  47.3 us
    pallas_call x1, Pallas kernels, inverse_factor(): pl.pallas_call(functools.partial(inverse_kernel, n, n_tp), out_shape=[jax...  32.3 us
    all_gather x1, blocking collectives, per_device(): basis_all = lax.all_gather(basis, 'fsdp', axis=1, tiled=True)  27.7 us
    all_to_all x3, starting transfers between devices, exchange(): lax.all_to_all(pieces, axis, 0, 0, tiled=True, axis_index_groups=index_gr...  15.8 us
    unnamed x23, local copies, waits for them, and re-layouts  12.5 us
    reduce_scatter x1, waiting for transfers between devices, per_device(): lax.psum_scatter(mine, 'fsdp', scatter_dimension=0, tiled=True, axis_inde...  7.14 us
    ppermute x1, starting transfers between devices, per_device(): other = lax.ppermute(own, 'fsdp', swap)  5.46 us
  transfers between devices with their start and end apart: 7, of which 6 were waited for; matrix products, arithmetic and copies ran while one was open for 1% of the time, Pallas kernels for 14%

profile of v3, /device:TPU:1, one launch (start us, length us, event | category | flops | bytes accessed | tf_op | source)
XLA Modules:
  0.0 248.2 jit_solution(8041456968117853327)
XLA Ops:
  7.2 27.7 %all_gather.6 = bf16[448,1024]{0,1:T(8,128)(2,1)S(1)} all-gather(bf16[448,64]{0,1:T(8,128)(2,1)} %param.5), channel_id=1, replica_groups=mesh['fsdp'=16,'tp'=32] {'fsdp'}, dimensions={1}, use_global_device_ids=true | all-gather | bytes 974848 | tf_op jit(solution)/shard_map/all_gather | solution.py:339
  34.9 1.3 fusion.4
  36.2 0.8 convolution_convert_fusion
  36.9 36.6 %all_to_all.30 = bf16[32,16,1024]{2,1,0:T(8,128)(2,1)S(1)} all-to-all(bf16[32,16,1024]{2,1,0:T(8,128)(2,1)S(1)} %bitcast.46), channel_id=1, replica_groups=mesh['fsdp'=16,'tp'=32] {'tp'}, dimensions={0} | all-to-all | bytes 2097152 | tf_op jit(solution)/shard_map/all_to_all | solution.py:25
  73.5 0.2 reduce_sum.39
  73.7 1.1 broadcast_in_dim.6
  74.8 5.9 %all-to-all-start.1 = ((bf16[32,16,1024]{2,1,0:T(8,128)(2,1)}), bf16[32,16,1024]{2,1,0:T(8,128)(2,1)S(1)}, u32[]{:S(2)}, u32[]{:S(2)}) async-start(bf16[32,16,1024]{2,1,0:T(8,128)(2,1)} %broadcast_in_dim.6), calls=%async_computation.1 | async-start | bytes 2097152 | tf_op jit(solution)/shard_map/all_to_all | solution.py:25
  80.6 0.0 reduce-scatter.2.cloned.1.call-start
  80.8 25.5 %all-to-all-done.1 = bf16[32,16,1024]{2,1,0:T(8,128)(2,1)S(1)} async-done(((bf16[32,16,1024]{2,1,0:T(8,128)(2,1)}), bf16[32,16,1024]{2,1,0:T(8,128)(2,1)S(1)}, u32[]{:S(2)}, u32[]{:S(2)}) %all-to-all-start.1) | async-done | bytes 1048608 | tf_op jit(solution)/shard_map/all_to_all | solution.py:25
  106.3 0.7 fusion.5
  107.0 0.1 dynamic-slice_bitcast_fusion
  107.1 5.3 %collective-permute-start = (f32[256,1024]{1,0:T(8,128)S(1)}, f32[256,1024]{1,0:T(8,128)S(1)}, u32[]{:S(2)}, u32[]{:S(2)}) collective-permute-start(f32[256,1024]{1,0:T(8,128)S(1)} %dynamic-slice_bitcast_fusion), channel_id=1, source_target_pairs={{0,32},{32,0},{64,96},{96,64},{128,160},{160,128},{192,224},{224,1... | collective-permute-start | bytes 3145736 | tf_op jit(solution)/shard_map/ppermute | solution.py:374
  112.4 0.4 fusion.8
  112.8 0.4 fusion.10
  113.1 1.5 collective-permute-done
  114.6 1.1 bitcast_add_fusion
  115.7 0.0 reduce-scatter.2.cloned.1.call-update
  115.8 3.8 %all_to_all.31 = f32[2,8,1152]{2,1,0:T(8,128)S(1)} all-to-all(f32[2,8,1152]{2,1,0:T(8,128)S(1)} %fusion.12), channel_id=1, replica_groups={{0,32},{64,96},{128,160},{192,224},{256,288},{320,352},{384,416},{448,4..., dimensions={0} | all-to-all | bytes 147456 | tf_op jit(solution)/shard_map/all_to_all | solution.py:25
  119.6 17.8 %all_to_all.32 = f32[8,8,1152]{2,1,0:T(8,128)S(1)} all-to-all(f32[8,8,1152]{2,1,0:T(8,128)S(1)} %broadcast_in_dim.7), channel_id=1, replica_groups={{0,64,128,192,256,320,384,448},{32,96,160,224,288,352,416,480},{1,65,12..., dimensions={0} | all-to-all | bytes 589824 | tf_op jit(solution)/shard_map/all_to_all | solution.py:25
  137.5 1.1 broadcast_in_dim.8
  138.6 4.6 %all-to-all-start.4 = ((f32[32,8,1152]{2,1,0:T(8,128)}), f32[32,8,1152]{2,1,0:T(8,128)S(1)}, u32[]{:S(2)}, u32[]{:S(2)}) async-start(f32[32,8,1152]{2,1,0:T(8,128)} %broadcast_in_dim.8), calls=%async_computation.5 | async-start | bytes 2359296 | tf_op jit(solution)/shard_map/all_to_all | solution.py:25
  143.2 0.0 all-gather.2.cloned.1.call-start
  143.3 7.1 %reduce-scatter.2.cloned.1.call-done = f32[32,1024]{1,0:T(8,128)} async-done(((f32[256,1024]{1,0:T(8,128)}), f32[32,1024]{1,0:T(8,128)}) %reduce-scatter.2.cloned.1.call-update) | async-done | bytes 131088 | tf_op jit(solution)/shard_map/reduce_scatter | solution.py:375
  150.4 0.0 all-gather.2.cloned.1.call-update
  150.4 21.2 %all-to-all-done.4.own_ref = f32[32,8,1152]{2,1,0:T(8,128)S(1)} async-done(((f32[32,8,1152]{2,1,0:T(8,128)}), f32[32,8,1152]{2,1,0:T(8,128)S(1)}, u32[]{:S(2)}, u32[]{:S(2)}) %all-to-all-start.4) | async-done | bytes 1179680 | tf_op jit(solution)/shard_map/all_to_all | solution.py:25
  171.6 5.5 %collective-permute-start.1 = (f32[32,8,1152]{2,1,0:T(8,128)S(1)}, f32[32,8,1152]{2,1,0:T(8,128)S(1)}, u32[]{:S(2)}, u32[]{:S(2)}) collective-permute-start(f32[32,8,1152]{2,1,0:T(8,128)S(1)} %all-to-all-done.4.own_ref), channel_id=1, source_target_pairs={{0,32},{32,0},{64,96},{96,64},{128,160},{160,128},{192,224},{224,1... | collective-permute-start | bytes 3538952 | tf_op jit(solution)/shard_map/ppermute | solution.py:364
  177.1 2.3 collective-permute-done.1.other_ref
  179.3 32.3 %shard_map.58 = (bf16[1024,1024]{1,0:T(8,128)(2,1)S(1)}, bf16[1024,1024]{1,0:T(8,128)(2,1)S(1)}) custom-call(s32[1]{0:T(128)} %bitcast.9.core_ref, f32[32,8,1152]{2,1,0:T(8,128)S(1)} %all-to-all-done.4.own_ref, f32[32,8,1152]{2,1,0:T(8,128)S(1)} %collective-permute-done.1.other_ref), custom_call_target="tpu_custom_call" | custom-call | flops 12884901888 | bytes 8388608 | tf_op jit(solution)/shard_map/pallas_call | solution.py:228
  211.7 0.0 copy-start.2
  211.7 1.3 copy-done.2
  213.0 1.3 copy-done.5
  214.3 1.6 copy-done.3
  215.9 1.6 copy-done.6
  217.5 1.6 copy-done.8
  219.1 4.7 %shard_map.59 = (f32[448,1024]{1,0:T(8,128)S(1)}, f32[32,1,1024]{2,1,0:T(1,128)}) custom-call(f32[512,1024]{1,0:T(8,128)S(1)} %copy-done.8, bf16[1024,1024]{1,0:T(8,128)(2,1)S(1)} %copy-done.3, bf16[1024,1024]{1,0:T(8,128)(2,1)S(1)} %copy-done.6), custom_call_target="tpu_custom_call" | custom-call | flops 2818572288 | bytes 3670016 | tf_op jit(solution)/shard_map/pallas_call | solution.py:280
  223.8 5.4 %all-to-all-start.5 = ((f32[32,1,1024]{2,1,0:T(1,128)}), f32[32,1,1024]{2,1,0:T(1,128)S(1)}, u32[]{:S(2)}, u32[]{:S(2)}) async-start(f32[32,1,1024]{2,1,0:T(1,128)} %get-tuple-element.14), calls=%async_computation.6 | async-start | bytes 262144 | tf_op jit(solution)/shard_map/all_to_all | solution.py:25
  229.2 1.6 copy-done.4
  230.8 1.6 copy-done.7
  232.3 3.1 %shard_map.60 = bf16[512,1024]{1,0:T(8,128)(2,1)S(1)} custom-call(bf16[512,1024]{1,0:T(8,128)(2,1)S(1)} %bitcast.43, bf16[1024,1024]{1,0:T(8,128)(2,1)S(1)} %copy-done.4, bf16[1024,1024]{1,0:T(8,128)(2,1)S(1)} %copy-done.7), custom_call_target="tpu_custom_call" | custom-call | tf_op jit(solution)/shard_map/pallas_call | solution.py:310
  235.5 1.0 copy-done
  236.4 1.5 fusion.2
  237.9 0.6 all-to-all-done.5
  238.5 0.1 reduce_sum.42
  238.6 0.2 divide_convert_fusion
  238.8 0.2 copy-done.1
  239.1 1.4 fusion.1
  240.5 0.1 constant_dynamic-slice_fusion
  240.7 0.7 copy.7
  (25 shorter events, 0.1 us)
Async XLA Ops:
  74.8 31.5 %all-to-all-start.1 = ((bf16[32,16,1024]{2,1,0:T(8,128)(2,1)}), bf16[32,16,1024]{2,1,0:T(8,128)(2,1)S(1)}, u32[]{:S(2)}, u32[]{:S(2)}) async-start(bf16[32,16,1024]{2,1,0:T(8,128)(2,1)} %broadcast_in_dim.6), calls=%async_computation.1 | async-start | bytes 2097152 | tf_op jit(solution)/shard_map/all_to_all | solution.py:25
  80.6 69.8 %reduce-scatter.2.cloned.1.call-start = ((), (), s32[]{:S(2)}) async-start(), calls=%async_computation.7 | async-start | bytes 1179648 | tf_op jit(solution)/shard_map/reduce_scatter | solution.py:375
  107.1 7.5 %collective-permute-start = (f32[256,1024]{1,0:T(8,128)S(1)}, f32[256,1024]{1,0:T(8,128)S(1)}, u32[]{:S(2)}, u32[]{:S(2)}) collective-permute-start(f32[256,1024]{1,0:T(8,128)S(1)} %dynamic-slice_bitcast_fusion), channel_id=1, source_target_pairs={{0,32},{32,0},{64,96},{96,64},{128,160},{160,128},{192,224},{224,1... | collective-permute-start | bytes 3145736 | tf_op jit(solution)/shard_map/ppermute | solution.py:374
  138.6 33.0 %all-to-all-start.4 = ((f32[32,8,1152]{2,1,0:T(8,128)}), f32[32,8,1152]{2,1,0:T(8,128)S(1)}, u32[]{:S(2)}, u32[]{:S(2)}) async-start(f32[32,8,1152]{2,1,0:T(8,128)} %broadcast_in_dim.8), calls=%async_computation.5 | async-start | bytes 2359296 | tf_op jit(solution)/shard_map/all_to_all | solution.py:25
  143.2 71.1 %all-gather.2.cloned.1.call-start = ((), (), s32[]{:S(2)}) async-start(), calls=%async_computation.8 | async-start | bytes 2228224 | tf_op jit(solution)/shard_map/all_gather | solution.py:378
  171.6 7.7 %collective-permute-start.1 = (f32[32,8,1152]{2,1,0:T(8,128)S(1)}, f32[32,8,1152]{2,1,0:T(8,128)S(1)}, u32[]{:S(2)}, u32[]{:S(2)}) collective-permute-start(f32[32,8,1152]{2,1,0:T(8,128)S(1)} %all-to-all-done.4.own_ref), channel_id=1, source_target_pairs={{0,32},{32,0},{64,96},{96,64},{128,160},{160,128},{192,224},{224,1... | collective-permute-start | bytes 3538952 | tf_op jit(solution)/shard_map/ppermute | solution.py:364
  211.7 1.3 copy-start.2
  213.0 1.3 copy-start.5
  214.3 1.6 copy-start.3
  215.9 1.6 copy-start.6
  217.5 1.6 copy-start.8
  223.8 14.7 %all-to-all-start.5 = ((f32[32,1,1024]{2,1,0:T(1,128)}), f32[32,1,1024]{2,1,0:T(1,128)S(1)}, u32[]{:S(2)}, u32[]{:S(2)}) async-start(f32[32,1,1024]{2,1,0:T(1,128)} %get-tuple-element.14), calls=%async_computation.6 | async-start | bytes 262144 | tf_op jit(solution)/shard_map/all_to_all | solution.py:25
  229.2 1.6 copy-start.4
  230.7 1.6 copy-start.7
  232.3 4.1 %copy-start.9 = (bf16[512,448]{0,1:T(8,128)(2,1)S(1)}, bf16[512,448]{0,1:T(8,128)(2,1)}, u32[]{:S(2)}) copy-start(bf16[512,448]{0,1:T(8,128)(2,1)} %param.4) | copy-start | bytes 1376260
  232.3 4.1 %copy-start.10 = (bf16[512,448]{0,1:T(8,128)(2,1)S(1)}, bf16[512,448]{0,1:T(8,128)(2,1)}, u32[]{:S(2)}) copy-start(bf16[512,448]{0,1:T(8,128)(2,1)} %param.3) | copy-start | bytes 1376260
  235.4 1.0 copy-start
  237.9 1.2 copy-start.1
Sparse Core Ops, SparseCore 0:
  115.9 34.4 reduce-scatter.1
  152.5 43.3 all-gather.1

commit v4 on v3

--- a/solution.py
+++ b/solution.py
@@ -11,6 +11,8 @@
 keep_rate = 0.95
 epsilon = 1e-06
 BLOCK = 128
+VM = 60 * 1024 * 1024
+VM1 = 60 * 1024 * 1024
 SUB = 8
 HI = lax.Precision.HIGHEST
 
@@ -230,7 +232,7 @@
         out_shape=[jax.ShapeDtypeStruct((rank, rank), jnp.bfloat16)] * 2,
         in_specs=[pl.BlockSpec(memory_space=pltpu.SMEM)]
         + [pl.BlockSpec(memory_space=pltpu.VMEM)] * 2,
-        out_specs=[pl.BlockSpec(memory_space=pl.ANY)] * 2,
+        out_specs=[pl.BlockSpec(memory_space=pltpu.HBM)] * 2,
         scratch_shapes=[
             pltpu.VMEM((rank, rank), jnp.float32),
             pltpu.VMEM((1, rank), jnp.float32),
@@ -240,7 +242,7 @@
             pltpu.VMEM((rank, rank), jnp.bfloat16),
             pltpu.SemaphoreType.DMA((2, n // 2)),
         ],
-        compiler_params=pltpu.CompilerParams(vmem_limit_bytes=32 * 1024 * 1024),
+        compiler_params=pltpu.CompilerParams(vmem_limit_bytes=VM1),
         cost_estimate=pl.CostEstimate(
             flops=12 * rank**3, bytes_accessed=8 * rank**2, transcendentals=0
         ),
@@ -290,32 +292,67 @@
             pl.BlockSpec((n_tp, 1, wide), lambda j: (0, 0, j)),
         ],
         scratch_shapes=[pltpu.VMEM((rows, rank), jnp.bfloat16)] * 2,
-        compiler_params=pltpu.CompilerParams(vmem_limit_bytes=24 * 1024 * 1024),
+        compiler_params=pltpu.CompilerParams(vmem_limit_bytes=VM),
         cost_estimate=pl.CostEstimate(
             flops=6 * rows * rank**2, bytes_accessed=8 * rank * rows, transcendentals=0
         ),
     )(back, high, low)
 
 
-def ortho_kernel(left_ref, high_ref, low_ref, ortho_ref):
-    total = dot16(left_ref[...], high_ref[...])
-    total += dot16(left_ref[...], low_ref[...])
-    ortho_ref[...] = total.astype(jnp.bfloat16)
-
-
-def orthonormal(left, high, low):
+def momentum_kernel(
+    left_ref, high_ref, low_ref, right_ref, momentum_ref, grad_ref, ortho_ref, out_ref, total
+):
+    step = pl.program_id(0)
+    ortho = dot16(left_ref[...], high_ref[...])
+    ortho += dot16(left_ref[...], low_ref[...])
+    ortho_b = ortho.astype(jnp.bfloat16)
+    ortho_ref[...] = ortho_b
+    change = dot16(right_ref[...].astype(jnp.bfloat16), ortho_b)
+
+    @pl.when(step == 0)
+    def _():
+        total[...] = change
+
+    @pl.when(step > 0)
+    def _():
+        total[...] += change
+
+    @pl.when(step == pl.num_programs(0) - 1)
+    def _():
+        kept = momentum_ref[...].astype(jnp.float32) + grad_ref[...].astype(jnp.float32)
+        out_ref[...] = (kept - (1.0 - keep_rate) * total[...]).astype(jnp.bfloat16)
+
+
+def new_momentum(left, high, low, right, momentum, grad):
     rows, rank = left.shape
+    cols = right.shape[0]
     wide = 2 * BLOCK
     block = pl.BlockSpec((wide, rank), lambda j: (j, 0))
+    whole = pl.BlockSpec((cols, rows), lambda j: (0, 0))
     return pl.pallas_call(
-        ortho_kernel,
-        out_shape=jax.ShapeDtypeStruct((rows, rank), jnp.bfloat16),
+        momentum_kernel,
+        out_shape=[
+            jax.ShapeDtypeStruct((rows, rank), jnp.bfloat16),
+            jax.ShapeDtypeStruct((cols, rows), jnp.bfloat16),
+        ],
         grid=(rank // wide,),
-        in_specs=[pl.BlockSpec(left.shape, lambda j: (0, 0)), block, block],
-        out_specs=pl.BlockSpec((rows, wide), lambda j: (0, j)),
-        compiler_params=pltpu.CompilerParams(vmem_limit_bytes=24 * 1024 * 1024),
-        cost_estimate=pl.CostEstimate(flops=0, bytes_accessed=0, transcendentals=0),
-    )(left, high, low)
+        in_specs=[
+            pl.BlockSpec((rows, rank), lambda j: (0, 0)),
+            block,
+            block,
+            pl.BlockSpec((cols, wide), lambda j: (0, j)),
+            whole,
+            whole,
+        ],
+        out_specs=[pl.BlockSpec((rows, wide), lambda j: (0, j)), whole],
+        scratch_shapes=[pltpu.VMEM((cols, rows), jnp.float32)],
+        compiler_params=pltpu.CompilerParams(vmem_limit_bytes=VM),
+        cost_estimate=pl.CostEstimate(
+            flops=4 * rows * rank**2 + 2 * rows * cols * rank,
+            bytes_accessed=10 * rank * rows,
+            transcendentals=0,
+        ),
+    )(left, high, low, right, momentum.T, grad.T)
 
 
 def per_device(momentum, grad, basis):
@@ -357,12 +394,6 @@
             for p in range(n // 2)
         ],
     )
-    packed = packed.reshape(2, strip // 2, packed.shape[1])
-    packed = jnp.sum(exchange(packed, "fsdp", core_groups), axis=0)
-    packed = jnp.sum(collect(packed, "fsdp", n_z, z_groups), axis=0)
-    own = collect(packed, "tp", n_tp)
-    other = lax.ppermute(own, "fsdp", swap)
-
     core = me_fsdp % 2
     half = cols // 2
     chunk = -(-half // (32 * n_z)) * 32
@@ -371,27 +402,31 @@
     back = back.reshape(2, chunk * n_z, rank)
     theirs = lax.dynamic_index_in_dim(back, 1 - core, 0, False)
     mine = lax.dynamic_index_in_dim(back, core, 0, False)
-    mine = mine + lax.ppermute(theirs, "fsdp", swap)
+    theirs = lax.ppermute(theirs, "fsdp", swap)
+    packed = packed.reshape(2, strip // 2, packed.shape[1])
+    packed = jnp.sum(exchange(packed, "fsdp", core_groups), axis=0)
+    packed, theirs = lax.optimization_barrier((packed, theirs))
+    mine = mine + theirs
     mine = lax.psum_scatter(
         mine, "fsdp", scatter_dimension=0, tiled=True, axis_index_groups=z_groups
     )
     back = lax.all_gather(mine, "fsdp", axis=0, tiled=True)
 
+    packed = jnp.sum(collect(packed, "fsdp", n_z, z_groups), axis=0)
+    own = collect(packed, "tp", n_tp)
+    other = lax.ppermute(own, "fsdp", swap)
+
     parity = core.astype(jnp.int32).reshape(1)
     inverse_high, inverse_low = inverse_factor(parity, own, other, rank)
     right, squares = project(back, inverse_high, inverse_low, cols, chunk, n_tp)
-    left, squares = lax.optimization_barrier((left, squares))
     squares = exchange(squares, "tp")
-    ortho_b = orthonormal(left, inverse_high, inverse_low)
+    ortho_b, kept = new_momentum(left, inverse_high, inverse_low, right, momentum, grad)
     scale = jnp.sqrt(jnp.sum(squares, axis=(0, 1)) / cols_all + epsilon)
-    right_b = right.astype(jnp.bfloat16)
     basis_full = (right / scale[None, :]).astype(jnp.bfloat16)
     basis_new = lax.dynamic_slice_in_dim(basis_full, me_fsdp * share, share, 1)
-    correction = dot(ortho_b, right_b, by_cols)
     raw = dot(ortho_b, basis_full, by_cols)
-    momentum_new = (total - (1.0 - keep_rate) * correction).astype(jnp.bfloat16)
     update = (math.sqrt(rows_all / rank) * raw).astype(jnp.bfloat16)
-    return (momentum_new, basis_new, update)
+    return (kept.T, basis_new, update)
 
 
 def solution(mesh):

time: 249 us -> 246 us (0.988)
  Pallas kernels: 40.1 us -> 50.7 us
  local copies, waits for them, and re-layouts: 15 us -> 5.32 us
  blocking collectives: 85.9 us -> 83.2 us
    unnamed x23 -> x13, local copies, waits for them, and re-layouts: 12.5 us -> 1.93 us
    pallas_call x1, Pallas kernels: 3.09 us -> 8.54 us  [new_momentum(): pl.pallas_call(momentum_kernel, out_shape=[jax.ShapeDtypeStruct((rows, ra...]
    all_to_all x3, blocking collectives: 58.2 us -> 55.4 us  [exchange(): lax.all_to_all(pieces, axis, 0, 0, tiled=True, axis_index_groups=index_gr...]
    all_to_all x3, waiting for transfers between devices: 47.3 us -> 44.7 us  [exchange(): lax.all_to_all(pieces, axis, 0, 0, tiled=True, axis_index_groups=index_gr...]
    pallas_call x1, Pallas kernels: 4.69 us -> 7.27 us  [project(): pl.pallas_call(functools.partial(right_kernel, chunk), out_shape=[jax.Sha...]
    pallas_call x1, Pallas kernels: 32.3 us -> 34.9 us  [inverse_factor(): pl.pallas_call(functools.partial(inverse_kernel, n, n_tp), out_shape=[jax...]
  transfers between devices with their start and end apart: 7 -> 7, of which waited for: 6 -> 5; matrix products, arithmetic and copies ran while one was open for 1% -> 0% of each run, Pallas kernels for 14% -> 18%
where the time goes in v4:
time: 246 us; the launch traced here: 245 us
  blocking collectives  83.2 us (34%)
  waiting for transfers between devices  56.6 us (23%)
  Pallas kernels  50.7 us (21%)
  starting transfers between devices  27.4 us (11%)
  between operations  14.3 us (6%)
  local copies, waits for them, and re-layouts  5.32 us (2%)
  matrix products  4.69 us (2%)
  other arithmetic  2.93 us (1%)
    all_to_all x3, blocking collectives, exchange(): lax.all_to_all(pieces, axis, 0, 0, tiled=True, axis_index_groups=index_gr...  55.4 us
    all_to_all x3, waiting for transfers between devices, exchange(): lax.all_to_all(pieces, axis, 0, 0, tiled=True, axis_index_groups=index_gr...  44.7 us
    pallas_call x1, Pallas kernels, inverse_factor(): pl.pallas_call(functools.partial(inverse_kernel, n, n_tp), out_shape=[jax...  34.9 us
    all_gather x1, blocking collectives, per_device(): basis_all = lax.all_gather(basis, 'fsdp', axis=1, tiled=True)  27.7 us
    all_to_all x3, starting transfers between devices, exchange(): lax.all_to_all(pieces, axis, 0, 0, tiled=True, axis_index_groups=index_gr...  16.3 us
    reduce_scatter x1, waiting for transfers between devices, per_device(): lax.psum_scatter(mine, 'fsdp', scatter_dimension=0, tiled=True, axis_inde...  9.57 us
    pallas_call x1, Pallas kernels, new_momentum(): pl.pallas_call(momentum_kernel, out_shape=[jax.ShapeDtypeStruct((rows, ra...  8.54 us
    pallas_call x1, Pallas kernels, project(): pl.pallas_call(functools.partial(right_kernel, chunk), out_shape=[jax.Sha...  7.27 us
  transfers between devices with their start and end apart: 7, of which 5 were waited for; matrix products, arithmetic and copies ran while one was open for 0% of the time, Pallas kernels for 18%

profile of v4, /device:TPU:1, one launch (start us, length us, event | category | flops | bytes accessed | tf_op | source)
XLA Modules:
  0.0 245.1 jit_solution(2766025267787546284)
XLA Ops:
  7.2 27.7 %all_gather.6 = bf16[448,1024]{0,1:T(8,128)(2,1)S(1)} all-gather(bf16[448,64]{0,1:T(8,128)(2,1)} %param.5), channel_id=1, replica_groups=mesh['fsdp'=16,'tp'=32] {'fsdp'}, dimensions={1}, use_global_device_ids=true | all-gather | bytes 974848 | tf_op jit(solution)/shard_map/all_gather | solution.py:376
  34.9 1.3 add_convert_fusion
  36.2 0.0 copy-start.2
  36.2 0.8 convolution_convert_fusion
  37.0 36.6 %all_to_all.30 = bf16[32,16,1024]{2,1,0:T(8,128)(2,1)S(1)} all-to-all(bf16[32,16,1024]{2,1,0:T(8,128)(2,1)S(1)} %bitcast.48), channel_id=1, replica_groups=mesh['fsdp'=16,'tp'=32] {'tp'}, dimensions={0} | all-to-all | bytes 2097152 | tf_op jit(solution)/shard_map/all_to_all | solution.py:27
  73.5 0.0 copy-done.2
  73.5 0.2 reduce_sum.39
  73.7 1.1 broadcast_in_dim.6
  74.8 5.9 %all-to-all-start.1 = ((bf16[32,16,1024]{2,1,0:T(8,128)(2,1)}), bf16[32,16,1024]{2,1,0:T(8,128)(2,1)S(1)}, u32[]{:S(2)}, u32[]{:S(2)}) async-start(bf16[32,16,1024]{2,1,0:T(8,128)(2,1)} %broadcast_in_dim.6), calls=%async_computation.1 | async-start | bytes 2097152 | tf_op jit(solution)/shard_map/all_to_all | solution.py:27
  80.7 0.0 reduce-scatter.2.cloned.1.call-start
  80.8 25.5 %all-to-all-done.1 = bf16[32,16,1024]{2,1,0:T(8,128)(2,1)S(1)} async-done(((bf16[32,16,1024]{2,1,0:T(8,128)(2,1)}), bf16[32,16,1024]{2,1,0:T(8,128)(2,1)S(1)}, u32[]{:S(2)}, u32[]{:S(2)}) %all-to-all-start.1) | async-done | bytes 1048608 | tf_op jit(solution)/shard_map/all_to_all | solution.py:27
  106.3 0.0 copy-start
  106.3 0.4 fusion.4
  106.7 0.4 fusion.6
  107.0 1.7 fusion.1
  108.8 0.0 copy-done
  108.8 1.0 dynamic-slice_bitcast_fusion
  109.8 5.3 %collective-permute-start = (f32[256,1024]{1,0:T(8,128)}, f32[256,1024]{1,0:T(8,128)S(1)}, u32[]{:S(2)}, u32[]{:S(2)}) collective-permute-start(f32[256,1024]{1,0:T(8,128)} %dynamic-slice_bitcast_fusion), channel_id=1, source_target_pairs={{0,32},{32,0},{64,96},{96,64},{128,160},{160,128},{192,224},{224,1... | collective-permute-start | bytes 3145736 | tf_op jit(solution)/shard_map/ppermute | solution.py:405
  115.2 3.4 %all_to_all.31 = f32[2,8,1152]{2,1,0:T(8,128)S(1)} all-to-all(f32[2,8,1152]{2,1,0:T(8,128)S(1)} %fusion.8), channel_id=1, replica_groups={{0,32},{64,96},{128,160},{192,224},{256,288},{320,352},{384,416},{448,4..., dimensions={0} | all-to-all | bytes 147456 | tf_op jit(solution)/shard_map/all_to_all | solution.py:27
  118.6 0.0 collective-permute-done
  118.6 1.1 bitcast_add_fusion
  119.7 0.0 reduce-scatter.2.cloned.1.call-update
  119.8 15.5 %all_to_all.32 = f32[8,8,1152]{2,1,0:T(8,128)S(1)} all-to-all(f32[8,8,1152]{2,1,0:T(8,128)S(1)} %broadcast_in_dim.7), channel_id=1, replica_groups={{0,64,128,192,256,320,384,448},{32,96,160,224,288,352,416,480},{1,65,12..., dimensions={0} | all-to-all | bytes 589824 | tf_op jit(solution)/shard_map/all_to_all | solution.py:27
  135.3 1.1 broadcast_in_dim.8
  136.4 5.1 %all-to-all-start.4 = ((f32[32,8,1152]{2,1,0:T(8,128)}), f32[32,8,1152]{2,1,0:T(8,128)S(1)}, u32[]{:S(2)}, u32[]{:S(2)}) async-start(f32[32,8,1152]{2,1,0:T(8,128)} %broadcast_in_dim.8), calls=%async_computation.4 | async-start | bytes 2359296 | tf_op jit(solution)/shard_map/all_to_all | solution.py:27
  141.5 0.0 all-gather.2.cloned.1.call-start
  141.5 9.6 %reduce-scatter.2.cloned.1.call-done = f32[32,1024]{1,0:T(8,128)} async-done(((f32[256,1024]{1,0:T(8,128)}), f32[32,1024]{1,0:T(8,128)}) %reduce-scatter.2.cloned.1.call-update) | async-done | bytes 131088 | tf_op jit(solution)/shard_map/reduce_scatter | solution.py:410
  151.1 0.0 all-gather.2.cloned.1.call-update
  151.1 18.4 %all-to-all-done.4.own_ref = f32[32,8,1152]{2,1,0:T(8,128)S(1)} async-done(((f32[32,8,1152]{2,1,0:T(8,128)}), f32[32,8,1152]{2,1,0:T(8,128)S(1)}, u32[]{:S(2)}, u32[]{:S(2)}) %all-to-all-start.4) | async-done | bytes 1179680 | tf_op jit(solution)/shard_map/all_to_all | solution.py:27
  169.5 0.0 copy-start.3
  169.5 5.8 %collective-permute-start.1 = (f32[32,8,1152]{2,1,0:T(8,128)S(1)}, f32[32,8,1152]{2,1,0:T(8,128)S(1)}, u32[]{:S(2)}, u32[]{:S(2)}) collective-permute-start(f32[32,8,1152]{2,1,0:T(8,128)S(1)} %all-to-all-done.4.own_ref), channel_id=1, source_target_pairs={{0,32},{32,0},{64,96},{96,64},{128,160},{160,128},{192,224},{224,1... | collective-permute-start | bytes 3538952 | tf_op jit(solution)/shard_map/ppermute | solution.py:417
  175.3 2.3 collective-permute-done.1.other_ref
  177.6 0.0 copy-done.3
  177.6 1.1 copy-done.4
  178.7 34.9 %shard_map.58 = (bf16[1024,1024]{1,0:T(8,128)(2,1)}, bf16[1024,1024]{1,0:T(8,128)(2,1)}) custom-call(s32[1]{0:T(128)} %bitcast.2.core_ref, f32[32,8,1152]{2,1,0:T(8,128)} %copy-done.3, f32[32,8,1152]{2,1,0:T(8,128)} %copy-done.4), custom_call_target="tpu_custom_call" | custom-call | flops 12884901888 | bytes 8388608 | tf_op jit(solution)/shard_map/pallas_call | solution.py:230
  213.5 0.0 all-gather.2.cloned.1.call-done.back_ref
  213.6 7.3 %shard_map.59 = (f32[448,1024]{1,0:T(8,128)}, f32[32,1,1024]{2,1,0:T(1,128)}) custom-call(f32[512,1024]{1,0:T(8,128)} %all-gather.2.cloned.1.call-done.back_ref, bf16[1024,1024]{1,0:T(8,128)(2,1)} %get-tuple-element.12.high_ref, bf16[1024,1024]{1,0:T(8,128)(2,1)} %get-tuple-element.13.low_ref), custom_call_target="tpu_custom_call" | custom-call | flops 2818572288 | bytes 3670016 | tf_op jit(solution)/shard_map/pallas_call | solution.py:282
  220.8 5.3 %all-to-all-start.5 = ((f32[32,1,1024]{2,1,0:T(1,128)}), f32[32,1,1024]{2,1,0:T(1,128)S(1)}, u32[]{:S(2)}, u32[]{:S(2)}) async-start(f32[32,1,1024]{2,1,0:T(1,128)} %get-tuple-element.17), calls=%async_computation.6 | async-start | bytes 262144 | tf_op jit(solution)/shard_map/all_to_all | solution.py:27
  226.2 0.0 copy-start.1
  226.2 8.5 %shard_map.60 = (bf16[512,1024]{1,0:T(8,128)(2,1)}, bf16[448,512]{1,0:T(8,128)(2,1)}) custom-call(bf16[512,1024]{1,0:T(8,128)(2,1)} %bitcast.45, bf16[1024,1024]{1,0:T(8,128)(2,1)} %get-tuple-element.12.high_ref, bf16[1024,1024]{1,0:T(8,128)(2,1)} %get-tuple-element.13.low_ref, f32[448,1024]{1,0:T(8,128)} %get-tuple-element.15.right_ref, ...), custom_call_target="tpu_custom_call" | custom-call | flops 2617245696 | bytes 5242880 | tf_op jit(solution)/shard_map/pallas_call | solution.py:332
  234.7 0.8 all-to-all-done.5
  235.5 0.1 reduce_sum.42
  235.6 0.0 copy-done.1
  235.6 0.2 divide_convert_fusion
  235.9 0.1 copy-done.5
  236.0 1.5 fusion
  237.4 0.1 constant_dynamic-slice_fusion
  237.5 0.7 copy.7
  (14 shorter events, 0.1 us)
Async XLA Ops:
  36.2 37.4 %copy-start.2 = (bf16[512,448]{0,1:T(8,128)(2,1)}, bf16[512,448]{0,1:T(8,128)(2,1)S(1)}, u32[]{:S(2)}) copy-start(bf16[512,448]{0,1:T(8,128)(2,1)S(1)} %add_convert_fusion) | copy-start | bytes 1376260
  74.8 31.5 %all-to-all-start.1 = ((bf16[32,16,1024]{2,1,0:T(8,128)(2,1)}), bf16[32,16,1024]{2,1,0:T(8,128)(2,1)S(1)}, u32[]{:S(2)}, u32[]{:S(2)}) async-start(bf16[32,16,1024]{2,1,0:T(8,128)(2,1)} %broadcast_in_dim.6), calls=%async_computation.1 | async-start | bytes 2097152 | tf_op jit(solution)/shard_map/all_to_all | solution.py:27
  80.7 70.4 %reduce-scatter.2.cloned.1.call-start = ((), (), s32[]{:S(2)}) async-start(), calls=%async_computation.7 | async-start | bytes 1179648 | tf_op jit(solution)/shard_map/reduce_scatter | solution.py:410
  106.3 2.5 %copy-start = (bf16[32,16,1024]{2,1,0:T(8,128)(2,1)}, bf16[32,16,1024]{2,1,0:T(8,128)(2,1)S(1)}, u32[]{:S(2)}) copy-start(bf16[32,16,1024]{2,1,0:T(8,128)(2,1)S(1)} %all-to-all-done.1) | copy-start | bytes 3145732
  109.8 8.8 %collective-permute-start = (f32[256,1024]{1,0:T(8,128)}, f32[256,1024]{1,0:T(8,128)S(1)}, u32[]{:S(2)}, u32[]{:S(2)}) collective-permute-start(f32[256,1024]{1,0:T(8,128)} %dynamic-slice_bitcast_fusion), channel_id=1, source_target_pairs={{0,32},{32,0},{64,96},{96,64},{128,160},{160,128},{192,224},{224,1... | collective-permute-start | bytes 3145736 | tf_op jit(solution)/shard_map/ppermute | solution.py:405
  136.4 33.1 %all-to-all-start.4 = ((f32[32,8,1152]{2,1,0:T(8,128)}), f32[32,8,1152]{2,1,0:T(8,128)S(1)}, u32[]{:S(2)}, u32[]{:S(2)}) async-start(f32[32,8,1152]{2,1,0:T(8,128)} %broadcast_in_dim.8), calls=%async_computation.4 | async-start | bytes 2359296 | tf_op jit(solution)/shard_map/all_to_all | solution.py:27
  141.5 72.1 %all-gather.2.cloned.1.call-start = ((), (), s32[]{:S(2)}) async-start(), calls=%async_computation.8 | async-start | bytes 2228224 | tf_op jit(solution)/shard_map/all_gather | solution.py:413
  169.5 8.1 %copy-start.3 = (f32[32,8,1152]{2,1,0:T(8,128)}, f32[32,8,1152]{2,1,0:T(8,128)S(1)}, u32[]{:S(2)}) copy-start(f32[32,8,1152]{2,1,0:T(8,128)S(1)} %all-to-all-done.4.own_ref) | copy-start | bytes 3538948
  169.5 8.1 %collective-permute-start.1 = (f32[32,8,1152]{2,1,0:T(8,128)S(1)}, f32[32,8,1152]{2,1,0:T(8,128)S(1)}, u32[]{:S(2)}, u32[]{:S(2)}) collective-permute-start(f32[32,8,1152]{2,1,0:T(8,128)S(1)} %all-to-all-done.4.own_ref), channel_id=1, source_target_pairs={{0,32},{32,0},{64,96},{96,64},{128,160},{160,128},{192,224},{224,1... | collective-permute-start | bytes 3538952 | tf_op jit(solution)/shard_map/ppermute | solution.py:417
  177.6 1.1 copy-start.4
  220.8 14.7 %all-to-all-start.5 = ((f32[32,1,1024]{2,1,0:T(1,128)}), f32[32,1,1024]{2,1,0:T(1,128)S(1)}, u32[]{:S(2)}, u32[]{:S(2)}) async-start(f32[32,1,1024]{2,1,0:T(1,128)} %get-tuple-element.17), calls=%async_computation.6 | async-start | bytes 262144 | tf_op jit(solution)/shard_map/all_to_all | solution.py:27
  226.2 9.5 %copy-start.1 = (f32[448,1024]{1,0:T(8,128)S(1)}, f32[448,1024]{1,0:T(8,128)}, u32[]{:S(2)}) copy-start(f32[448,1024]{1,0:T(8,128)} %get-tuple-element.15.right_ref) | copy-start | bytes 5505028
  234.7 1.2 copy-start.5
Sparse Core Ops, SparseCore 0:
  119.9 31.1 reduce-scatter.1
  153.2 45.1 all-gather.1

commit v5 on v4

--- a/solution.py
+++ b/solution.py
@@ -12,9 +12,9 @@
 epsilon = 1e-06
 BLOCK = 128
 VM = 60 * 1024 * 1024
-VM1 = 60 * 1024 * 1024
+VM1 = 51 * 1024 * 1024
 SUB = 8
-HI = lax.Precision.HIGHEST
+HI = lax.Precision.HIGH
 
 
 def groups(n_fsdp):
@@ -355,6 +355,56 @@
     )(left, high, low, right, momentum.T, grad.T)
 
 
+def by_rows(a, b):
+    return lax.dot_general(a, b, (((0,), (0,)), ((), ())), preferred_element_type=jnp.float32)
+
+
+def left_kernel(n, place_ref, left_ref, spread_ref, packed_ref, mine_ref, theirs_ref, strips):
+    pair, offset, core = place_ref[0], place_ref[1], place_ref[2]
+    half = packed_ref.shape[1]
+    for s, row in enumerate((pair, n - 1 - pair)):
+        lanes = pl.ds(pl.multiple_of(row * BLOCK, BLOCK), BLOCK)
+        strips[s] = by_rows(left_ref[:, lanes], left_ref[...])
+    for p in range(n // 2):
+
+        @pl.when(pair == p)
+        def _():
+            width = (n - p) * BLOCK
+            for h in range(2):
+                rows = pl.ds(pl.multiple_of(offset + h * half, half), half)
+                packed_ref[h, :, :width] = strips[0, rows, p * BLOCK :]
+                packed_ref[h, :, width:] = strips[1, rows, (n - 1 - p) * BLOCK :]
+
+    wide = mine_ref.shape[0]
+    for target, part in ((theirs_ref, 1 - core), (mine_ref, core)):
+        lanes = pl.ds(pl.multiple_of(part * wide, wide), wide)
+        target[...] = by_rows(spread_ref[:, lanes], left_ref[...])
+
+
+def from_left(where, left, spread, n, strip):
+    rank = left.shape[1]
+    wide = spread.shape[1] // 2
+    half = jax.ShapeDtypeStruct((wide, rank), jnp.float32)
+    return pl.pallas_call(
+        functools.partial(left_kernel, n),
+        out_shape=[
+            jax.ShapeDtypeStruct((2, strip // 2, (n + 1) * BLOCK), jnp.float32),
+            half,
+            half,
+        ],
+        in_specs=[pl.BlockSpec(memory_space=pltpu.SMEM)]
+        + [pl.BlockSpec(memory_space=pltpu.VMEM)] * 2,
+        out_specs=[pl.BlockSpec(memory_space=pltpu.VMEM)] * 3,
+        scratch_shapes=[pltpu.VMEM((2, BLOCK, rank), jnp.float32)],
+        compiler_params=pltpu.CompilerParams(vmem_limit_bytes=16 * 1024 * 1024),
+        cost_estimate=pl.CostEstimate(
+            flops=2 * left.shape[0] * rank * (2 * BLOCK + 2 * wide),
+            bytes_accessed=8 * rank * left.shape[0],
+            transcendentals=0,
+        ),
+    )(where, left, spread)
+
+
 def per_device(momentum, grad, basis):
     n_fsdp, n_tp = lax.axis_size("fsdp"), lax.axis_size("tp")
     n_z = n_fsdp // 2
@@ -365,7 +415,6 @@
     rank = share * n_fsdp
     rows_all, cols_all = rows * n_fsdp, cols * n_tp
     me_fsdp, me_tp = lax.axis_index("fsdp"), lax.axis_index("tp")
-    by_rows = (((0,), (0,)), ((), ()))
     by_cols = (((1,), (1,)), ((), ()))
 
     def dot(a, b, dims):
@@ -382,28 +431,14 @@
     n = rank // BLOCK
     per_pair = n_tp // (n // 2)
     strip = BLOCK // per_pair
-    pair, mirror, offset = place(me_tp, per_pair, n, strip)
-    made = []
-    for row in (pair, mirror):
-        mine = lax.dynamic_slice_in_dim(left, row * BLOCK + offset, strip, 1)
-        made.append(dot(mine, left, by_rows))
-    packed = lax.select_n(
-        pair,
-        *[
-            jnp.concatenate([made[0][:, p * BLOCK :], made[1][:, (n - 1 - p) * BLOCK :]], axis=1)
-            for p in range(n // 2)
-        ],
-    )
+    pair, _, offset = place(me_tp, per_pair, n, strip)
     core = me_fsdp % 2
     half = cols // 2
     chunk = -(-half // (32 * n_z)) * 32
     spread = jnp.pad(total_b.reshape(rows, 2, half), ((0, 0), (0, 0), (0, chunk * n_z - half)))
-    back = dot(spread.reshape(rows, 2 * chunk * n_z), left, by_rows)
-    back = back.reshape(2, chunk * n_z, rank)
-    theirs = lax.dynamic_index_in_dim(back, 1 - core, 0, False)
-    mine = lax.dynamic_index_in_dim(back, core, 0, False)
+    where = jnp.stack([pair, offset, core]).astype(jnp.int32)
+    packed, mine, theirs = from_left(where, left, spread.reshape(rows, 2 * chunk * n_z), n, strip)
     theirs = lax.ppermute(theirs, "fsdp", swap)
-    packed = packed.reshape(2, strip // 2, packed.shape[1])
     packed = jnp.sum(exchange(packed, "fsdp", core_groups), axis=0)
     packed, theirs = lax.optimization_barrier((packed, theirs))
     mine = mine + theirs

time: 246 us -> 239 us (0.972)
  matrix products: 4.69 us -> 2.23 us
    pallas_call x1, Pallas kernels: 34.9 us -> 30.2 us  [inverse_factor(): pl.pallas_call(functools.partial(inverse_kernel, n, n_tp), out_shape=[jax...]
    pallas_call x0 -> x1, Pallas kernels: none -> 2.49 us  [from_left(): pl.pallas_call(functools.partial(left_kernel, n), out_shape=[jax.ShapeDty...]
  transfers between devices with their start and end apart: 7 -> 7, of which waited for: 5 -> 5; matrix products, arithmetic and copies ran while one was open for 0% -> 1% of each run, Pallas kernels for 18% -> 16%
where the time goes in v5:
time: 239 us; the launch traced here: 238 us
  blocking collectives  83.1 us (35%)
  waiting for transfers between devices  55.5 us (23%)
  Pallas kernels  48.5 us (20%)
  starting transfers between devices  27.5 us (12%)
  between operations  14.2 us (6%)
  local copies, waits for them, and re-layouts  4.16 us (2%)
  other arithmetic  3 us (1%)
    all_to_all x3, blocking collectives, exchange(): lax.all_to_all(pieces, axis, 0, 0, tiled=True, axis_index_groups=index_gr...  55.4 us
    all_to_all x3, waiting for transfers between devices, exchange(): lax.all_to_all(pieces, axis, 0, 0, tiled=True, axis_index_groups=index_gr...  44 us
    pallas_call x1, Pallas kernels, inverse_factor(): pl.pallas_call(functools.partial(inverse_kernel, n, n_tp), out_shape=[jax...  30.2 us
    all_gather x1, blocking collectives, per_device(): basis_all = lax.all_gather(basis, 'fsdp', axis=1, tiled=True)  27.7 us
    all_to_all x3, starting transfers between devices, exchange(): lax.all_to_all(pieces, axis, 0, 0, tiled=True, axis_index_groups=index_gr...  16.3 us
    reduce_scatter x1, waiting for transfers between devices, per_device(): lax.psum_scatter(mine, 'fsdp', scatter_dimension=0, tiled=True, axis_inde...  9.22 us
    pallas_call x1, Pallas kernels, new_momentum(): pl.pallas_call(momentum_kernel, out_shape=[jax.ShapeDtypeStruct((rows, ra...  8.55 us
    pallas_call x1, Pallas kernels, project(): pl.pallas_call(functools.partial(right_kernel, chunk), out_shape=[jax.Sha...  7.27 us
  transfers between devices with their start and end apart: 7, of which 5 were waited for; matrix products, arithmetic and copies ran while one was open for 1% of the time, Pallas kernels for 16%

profile of v5, /device:TPU:1, one launch (start us, length us, event | category | flops | bytes accessed | tf_op | source)
XLA Modules:
  0.0 238.2 jit_solution(10228163451485577658)
XLA Ops:
  7.2 27.7 %all_gather.6 = bf16[448,1024]{0,1:T(8,128)(2,1)S(1)} all-gather(bf16[448,64]{0,1:T(8,128)(2,1)} %param.5), channel_id=1, replica_groups=mesh['fsdp'=16,'tp'=32] {'fsdp'}, dimensions={1}, use_global_device_ids=true | all-gather | bytes 974848 | tf_op jit(solution)/shard_map/all_gather | solution.py:425
  34.9 1.3 add_convert_fusion
  36.2 0.8 convolution_convert_fusion
  36.9 36.6 %all_to_all.30 = bf16[32,16,1024]{2,1,0:T(8,128)(2,1)S(1)} all-to-all(bf16[32,16,1024]{2,1,0:T(8,128)(2,1)S(1)} %bitcast.20), channel_id=1, replica_groups=mesh['fsdp'=16,'tp'=32] {'tp'}, dimensions={0} | all-to-all | bytes 2097152 | tf_op jit(solution)/shard_map/all_to_all | solution.py:27
  73.5 0.2 reduce_sum.39
  73.7 1.1 broadcast_in_dim.6
  74.8 5.9 %all-to-all-start.1 = ((bf16[32,16,1024]{2,1,0:T(8,128)(2,1)}), bf16[32,16,1024]{2,1,0:T(8,128)(2,1)S(1)}, u32[]{:S(2)}, u32[]{:S(2)}) async-start(bf16[32,16,1024]{2,1,0:T(8,128)(2,1)} %broadcast_in_dim.6), calls=%async_computation.1 | async-start | bytes 2097152 | tf_op jit(solution)/shard_map/all_to_all | solution.py:27
  80.6 0.0 reduce-scatter.2.cloned.1.call-start
  80.7 0.4 copy.8
  81.2 0.5 pad.4
  81.7 0.1 copy.10
  81.8 0.1 pad_add_fusion.place_ref
  81.8 24.4 %all-to-all-done.1 = bf16[32,16,1024]{2,1,0:T(8,128)(2,1)S(1)} async-done(((bf16[32,16,1024]{2,1,0:T(8,128)(2,1)}), bf16[32,16,1024]{2,1,0:T(8,128)(2,1)S(1)}, u32[]{:S(2)}, u32[]{:S(2)}) %all-to-all-start.1) | async-done | bytes 1048608 | tf_op jit(solution)/shard_map/all_to_all | solution.py:27
  106.3 0.0 copy-start
  106.3 2.5 %shard_map.58 = (f32[2,8,1152]{2,1,0:T(8,128)S(1)}, f32[256,1024]{1,0:T(8,128)S(1)}, f32[256,1024]{1,0:T(8,128)}) custom-call(s32[3]{0:T(128)S(1)} %pad_add_fusion.place_ref, bf16[512,1024]{1,0:T(8,128)(2,1)S(1)} %bitcast.15, bf16[512,512]{1,0:T(8,128)(2,1)S(1)} %bitcast.17), custom_call_target="tpu_custom_call" | custom-call | flops 805306368 | bytes 4194304 | tf_op jit(solution)/shard_map/pallas_call | solution.py:388
  108.8 5.3 %collective-permute-start = (f32[256,1024]{1,0:T(8,128)}, f32[256,1024]{1,0:T(8,128)S(1)}, u32[]{:S(2)}, u32[]{:S(2)}) collective-permute-start(f32[256,1024]{1,0:T(8,128)} %get-tuple-element.15), channel_id=1, source_target_pairs={{0,32},{32,0},{64,96},{96,64},{128,160},{160,128},{192,224},{224,1... | collective-permute-start | bytes 3145736 | tf_op jit(solution)/shard_map/ppermute | solution.py:441
  114.0 3.4 %all_to_all.31 = f32[2,8,1152]{2,1,0:T(8,128)S(1)} all-to-all(f32[2,8,1152]{2,1,0:T(8,128)S(1)} %get-tuple-element.14), channel_id=1, replica_groups={{0,32},{64,96},{128,160},{192,224},{256,288},{320,352},{384,416},{448,4..., dimensions={0} | all-to-all | bytes 147456 | tf_op jit(solution)/shard_map/all_to_all | solution.py:27
  117.5 0.0 collective-permute-done
  117.5 1.1 add.34
  118.6 0.0 copy-done
  118.6 0.0 reduce-scatter.2.cloned.1.call-update
  118.7 15.4 %all_to_all.32 = f32[8,8,1152]{2,1,0:T(8,128)S(1)} all-to-all(f32[8,8,1152]{2,1,0:T(8,128)S(1)} %broadcast_in_dim.7), channel_id=1, replica_groups={{0,64,128,192,256,320,384,448},{32,96,160,224,288,352,416,480},{1,65,12..., dimensions={0} | all-to-all | bytes 589824 | tf_op jit(solution)/shard_map/all_to_all | solution.py:27
  134.1 1.1 broadcast_in_dim.8
  135.2 5.1 %all-to-all-start.4 = ((f32[32,8,1152]{2,1,0:T(8,128)}), f32[32,8,1152]{2,1,0:T(8,128)S(1)}, u32[]{:S(2)}, u32[]{:S(2)}) async-start(f32[32,8,1152]{2,1,0:T(8,128)} %broadcast_in_dim.8), calls=%async_computation.4 | async-start | bytes 2359296 | tf_op jit(solution)/shard_map/all_to_all | solution.py:27
  140.3 0.0 all-gather.2.cloned.1.call-start
  140.4 9.2 %reduce-scatter.2.cloned.1.call-done = f32[32,1024]{1,0:T(8,128)} async-done(((f32[256,1024]{1,0:T(8,128)}), f32[32,1024]{1,0:T(8,128)}) %reduce-scatter.2.cloned.1.call-update) | async-done | bytes 131088 | tf_op jit(solution)/shard_map/reduce_scatter | solution.py:445
  149.6 0.0 all-gather.2.cloned.1.call-update
  149.6 18.8 %all-to-all-done.4.own_ref = f32[32,8,1152]{2,1,0:T(8,128)S(1)} async-done(((f32[32,8,1152]{2,1,0:T(8,128)}), f32[32,8,1152]{2,1,0:T(8,128)S(1)}, u32[]{:S(2)}, u32[]{:S(2)}) %all-to-all-start.4) | async-done | bytes 1179680 | tf_op jit(solution)/shard_map/all_to_all | solution.py:27
  168.4 5.8 %collective-permute-start.1 = (f32[32,8,1152]{2,1,0:T(8,128)S(1)}, f32[32,8,1152]{2,1,0:T(8,128)S(1)}, u32[]{:S(2)}, u32[]{:S(2)}) collective-permute-start(f32[32,8,1152]{2,1,0:T(8,128)S(1)} %all-to-all-done.4.own_ref), channel_id=1, source_target_pairs={{0,32},{32,0},{64,96},{96,64},{128,160},{160,128},{192,224},{224,1... | collective-permute-start | bytes 3538952 | tf_op jit(solution)/shard_map/ppermute | solution.py:452
  174.2 2.3 collective-permute-done.1.other_ref
  176.4 30.2 %shard_map.59 = (bf16[1024,1024]{1,0:T(8,128)(2,1)}, bf16[1024,1024]{1,0:T(8,128)(2,1)}) custom-call(s32[1]{0:T(128)} %bitcast.2.core_ref, f32[32,8,1152]{2,1,0:T(8,128)S(1)} %all-to-all-done.4.own_ref, f32[32,8,1152]{2,1,0:T(8,128)S(1)} %collective-permute-done.1.other_ref), custom_call_target="tpu_custom_call" | custom-call | flops 12884901888 | bytes 8388608 | tf_op jit(solution)/shard_map/pallas_call | solution.py:230
  206.6 0.0 all-gather.2.cloned.1.call-done.back_ref
  206.6 7.3 %shard_map.60 = (f32[448,1024]{1,0:T(8,128)}, f32[32,1,1024]{2,1,0:T(1,128)}) custom-call(f32[512,1024]{1,0:T(8,128)} %all-gather.2.cloned.1.call-done.back_ref, bf16[1024,1024]{1,0:T(8,128)(2,1)} %get-tuple-element.17.high_ref, bf16[1024,1024]{1,0:T(8,128)(2,1)} %get-tuple-element.18.low_ref), custom_call_target="tpu_custom_call" | custom-call | flops 2818572288 | bytes 3670016 | tf_op jit(solution)/shard_map/pallas_call | solution.py:282
  213.9 5.4 %all-to-all-start.5 = ((f32[32,1,1024]{2,1,0:T(1,128)}), f32[32,1,1024]{2,1,0:T(1,128)S(1)}, u32[]{:S(2)}, u32[]{:S(2)}) async-start(f32[32,1,1024]{2,1,0:T(1,128)} %get-tuple-element.23), calls=%async_computation.6 | async-start | bytes 262144 | tf_op jit(solution)/shard_map/all_to_all | solution.py:27
  219.3 0.0 copy-start.1
  219.3 8.5 %shard_map.61 = (bf16[512,1024]{1,0:T(8,128)(2,1)}, bf16[448,512]{1,0:T(8,128)(2,1)}) custom-call(bf16[512,1024]{1,0:T(8,128)(2,1)} %bitcast.16, bf16[1024,1024]{1,0:T(8,128)(2,1)} %get-tuple-element.17.high_ref, bf16[1024,1024]{1,0:T(8,128)(2,1)} %get-tuple-element.18.low_ref, f32[448,1024]{1,0:T(8,128)} %get-tuple-element.21.right_ref, ...), custom_call_target="tpu_custom_call" | custom-call | flops 2617245696 | bytes 5242880 | tf_op jit(solution)/shard_map/pallas_call | solution.py:332
  227.8 0.0 copy-start.2
  227.8 0.8 all-to-all-done.5
  228.6 0.1 reduce_sum.42
  228.7 0.0 copy-done.1
  228.7 0.2 divide_convert_fusion
  229.0 0.1 copy-done.2
  229.1 1.5 fusion
  230.5 0.1 constant_dynamic-slice_fusion
  230.6 0.7 copy.9
  (4 shorter events, 0.1 us)
Async XLA Ops:
  74.8 31.5 %all-to-all-start.1 = ((bf16[32,16,1024]{2,1,0:T(8,128)(2,1)}), bf16[32,16,1024]{2,1,0:T(8,128)(2,1)S(1)}, u32[]{:S(2)}, u32[]{:S(2)}) async-start(bf16[32,16,1024]{2,1,0:T(8,128)(2,1)} %broadcast_in_dim.6), calls=%async_computation.1 | async-start | bytes 2097152 | tf_op jit(solution)/shard_map/all_to_all | solution.py:27
  80.6 68.9 %reduce-scatter.2.cloned.1.call-start = ((), (), s32[]{:S(2)}) async-start(), calls=%async_computation.7 | async-start | bytes 1179648 | tf_op jit(solution)/shard_map/reduce_scatter | solution.py:445
  106.3 12.3 %copy-start = (bf16[32,16,1024]{2,1,0:T(8,128)(2,1)}, bf16[32,16,1024]{2,1,0:T(8,128)(2,1)S(1)}, u32[]{:S(2)}) copy-start(bf16[32,16,1024]{2,1,0:T(8,128)(2,1)S(1)} %all-to-all-done.1) | copy-start | bytes 3145732
  108.8 8.7 %collective-permute-start = (f32[256,1024]{1,0:T(8,128)}, f32[256,1024]{1,0:T(8,128)S(1)}, u32[]{:S(2)}, u32[]{:S(2)}) collective-permute-start(f32[256,1024]{1,0:T(8,128)} %get-tuple-element.15), channel_id=1, source_target_pairs={{0,32},{32,0},{64,96},{96,64},{128,160},{160,128},{192,224},{224,1... | collective-permute-start | bytes 3145736 | tf_op jit(solution)/shard_map/ppermute | solution.py:441
  135.2 33.2 %all-to-all-start.4 = ((f32[32,8,1152]{2,1,0:T(8,128)}), f32[32,8,1152]{2,1,0:T(8,128)S(1)}, u32[]{:S(2)}, u32[]{:S(2)}) async-start(f32[32,8,1152]{2,1,0:T(8,128)} %broadcast_in_dim.8), calls=%async_computation.4 | async-start | bytes 2359296 | tf_op jit(solution)/shard_map/all_to_all | solution.py:27
  140.3 66.3 %all-gather.2.cloned.1.call-start = ((), (), s32[]{:S(2)}) async-start(), calls=%async_computation.8 | async-start | bytes 2228224 | tf_op jit(solution)/shard_map/all_gather | solution.py:448
  168.4 8.1 %collective-permute-start.1 = (f32[32,8,1152]{2,1,0:T(8,128)S(1)}, f32[32,8,1152]{2,1,0:T(8,128)S(1)}, u32[]{:S(2)}, u32[]{:S(2)}) collective-permute-start(f32[32,8,1152]{2,1,0:T(8,128)S(1)} %all-to-all-done.4.own_ref), channel_id=1, source_target_pairs={{0,32},{32,0},{64,96},{96,64},{128,160},{160,128},{192,224},{224,1... | collective-permute-start | bytes 3538952 | tf_op jit(solution)/shard_map/ppermute | solution.py:452
  213.9 14.7 %all-to-all-start.5 = ((f32[32,1,1024]{2,1,0:T(1,128)}), f32[32,1,1024]{2,1,0:T(1,128)S(1)}, u32[]{:S(2)}, u32[]{:S(2)}) async-start(f32[32,1,1024]{2,1,0:T(1,128)} %get-tuple-element.23), calls=%async_computation.6 | async-start | bytes 262144 | tf_op jit(solution)/shard_map/all_to_all | solution.py:27
  219.3 9.5 %copy-start.1 = (f32[448,1024]{1,0:T(8,128)S(1)}, f32[448,1024]{1,0:T(8,128)}, u32[]{:S(2)}) copy-start(f32[448,1024]{1,0:T(8,128)} %get-tuple-element.21.right_ref) | copy-start | bytes 5505028
  227.8 1.2 copy-start.2
Sparse Core Ops, SparseCore 0:
  118.8 30.7 reduce-scatter.1
  151.7 45.4 all-gather.1

commit v6 on v5

--- a/solution.py
+++ b/solution.py
@@ -139,25 +139,31 @@
     strip = BLOCK // per_pair
     half = strip // 2
     core = core_ref[0]
-    for t in range(n_tp):
-        first, second, offset = place(t, per_pair, n, strip)
-        width = (n - first) * BLOCK
-        for source, c in ((own_ref, core), (other_ref, 1 - core)):
-            for row, lanes in ((first, slice(0, width)), (second, slice(width, None))):
+
+    def load(row):
+        for t in range(n_tp):
+            first, second, offset = place(t, per_pair, n, strip)
+            if row not in (first, second):
+                continue
+            width = (n - first) * BLOCK
+            lanes = slice(0, width) if row == first else slice(width, None)
+            for source, c in ((own_ref, core), (other_ref, 1 - core)):
                 start = pl.multiple_of(row * BLOCK + offset + c * half, half)
                 work[pl.ds(start, half), row * BLOCK :] = source[t, :, lanes]
 
     r = lax.broadcasted_iota(jnp.int32, (BLOCK, BLOCK), 0)
     c = lax.broadcasted_iota(jnp.int32, (BLOCK, BLOCK), 1)
-    tall = []
-    for i in range(n):
-        rows = slice(i * BLOCK, (i + 1) * BLOCK)
+    tall = {}
+
+    def measure(row):
+        rows = slice(row * BLOCK, (row + 1) * BLOCK)
         diagonal = jnp.where(r == c, work[rows, rows], 0.0)
         scale[:, rows] = lax.rsqrt(jnp.sum(diagonal, axis=0, keepdims=True))
-        tall.append(lax.rsqrt(jnp.sum(diagonal, axis=1, keepdims=True)))
-    for i in range(n):
-        rows, rest = slice(i * BLOCK, (i + 1) * BLOCK), slice(i * BLOCK, None)
-        work[rows, rest] = work[rows, rest] * tall[i] * scale[:, rest]
+        tall[row] = lax.rsqrt(jnp.sum(diagonal, axis=1, keepdims=True))
+
+    def normalise(row, lanes):
+        rows = slice(row * BLOCK, (row + 1) * BLOCK)
+        work[rows, lanes] = work[rows, lanes] * tall[row] * scale[:, lanes]
 
     wide = 2 * BLOCK
     n_wide = n // 2
@@ -191,7 +197,16 @@
         for copy in copies(k):
             copy.start()
 
-    aside = []
+    for row in range(2):
+        load(row)
+        measure(row)
+    for row in range(2):
+        normalise(row, slice(row * BLOCK, wide))
+    aside = [functools.partial(load, row) for row in range(2, n)]
+    aside += [functools.partial(measure, row) for row in range(2, n)]
+    aside += [
+        functools.partial(normalise, row, slice(max(row, 2) * BLOCK, None)) for row in range(n)
+    ]
     for k in range(n_wide):
         here, corner = spans[k], corners.at[k % 2]
         top, bottom = slice(k * wide, k * wide + BLOCK), slice(k * wide + BLOCK, (k + 1) * wide)
@@ -265,18 +280,24 @@
             back_high[start : start + chunk, :] = high
             back_low[start : start + chunk, :] = low
 
-    total = dot16(back_high[...], high_ref[...])
-    total += dot16(back_high[...], low_ref[...])
-    total += dot16(back_low[...], high_ref[...])
-    right_ref[...] = total
-    squares = jnp.sum(total * total, axis=0, keepdims=True)
-    for t in range(squares_ref.shape[0]):
-        squares_ref[t] = squares
+    wide, rank = high_ref.shape
+    for j in range(rank // wide):
+
+        @pl.when(pl.program_id(0) == j)
+        def _():
+            depth = slice(0, (j + 1) * wide)
+            total = dot16(back_high[:, depth], high_ref[:, depth])
+            total += dot16(back_high[:, depth], low_ref[:, depth])
+            total += dot16(back_low[:, depth], high_ref[:, depth])
+            right_ref[...] = total
+            squares = jnp.sum(total * total, axis=0, keepdims=True)
+            for t in range(squares_ref.shape[0]):
+                squares_ref[t] = squares
 
 
 def project(back, high, low, rows, chunk, n_tp):
     rank = back.shape[1]
-    wide = 2 * BLOCK
+    wide = 4 * BLOCK
     whole = pl.BlockSpec(back.shape, lambda j: (0, 0))
     block = pl.BlockSpec((wide, rank), lambda j: (j, 0))
     return pl.pallas_call(
@@ -302,31 +323,31 @@
 def momentum_kernel(
     left_ref, high_ref, low_ref, right_ref, momentum_ref, grad_ref, ortho_ref, out_ref, total
 ):
-    step = pl.program_id(0)
-    ortho = dot16(left_ref[...], high_ref[...])
-    ortho += dot16(left_ref[...], low_ref[...])
-    ortho_b = ortho.astype(jnp.bfloat16)
-    ortho_ref[...] = ortho_b
-    change = dot16(right_ref[...].astype(jnp.bfloat16), ortho_b)
-
-    @pl.when(step == 0)
-    def _():
-        total[...] = change
-
-    @pl.when(step > 0)
-    def _():
-        total[...] += change
-
-    @pl.when(step == pl.num_programs(0) - 1)
-    def _():
-        kept = momentum_ref[...].astype(jnp.float32) + grad_ref[...].astype(jnp.float32)
-        out_ref[...] = (kept - (1.0 - keep_rate) * total[...]).astype(jnp.bfloat16)
+    wide, rank = high_ref.shape
+    steps = rank // wide
+    for j in range(steps):
+
+        @pl.when(pl.program_id(0) == j)
+        def _():
+            depth = slice(0, (j + 1) * wide)
+            ortho = dot16(left_ref[:, depth], high_ref[:, depth])
+            ortho += dot16(left_ref[:, depth], low_ref[:, depth])
+            ortho_b = ortho.astype(jnp.bfloat16)
+            ortho_ref[...] = ortho_b
+            change = dot16(right_ref[...].astype(jnp.bfloat16), ortho_b)
+            if j > 0:
+                change += total[...]
+            if j + 1 < steps:
+                total[...] = change
+            else:
+                kept = momentum_ref[...].astype(jnp.float32) + grad_ref[...].astype(jnp.float32)
+                out_ref[...] = (kept - (1.0 - keep_rate) * change).astype(jnp.bfloat16)
 
 
 def new_momentum(left, high, low, right, momentum, grad):
     rows, rank = left.shape
     cols = right.shape[0]
-    wide = 2 * BLOCK
+    wide = 4 * BLOCK
     block = pl.BlockSpec((wide, rank), lambda j: (j, 0))
     whole = pl.BlockSpec((cols, rows), lambda j: (0, 0))
     return pl.pallas_call(

time: 239 us -> 237 us (level)
  Pallas kernels: 48.5 us -> 45.3 us
  transfers between devices with their start and end apart: 7 -> 7, of which waited for: 5 -> 5; matrix products, arithmetic and copies ran while one was open for 1% -> 1% of each run, Pallas kernels for 16% -> 15%
where the time goes in v6:
time: 237 us
  blocking collectives  83.1 us (35%)
  waiting for transfers between devices  57.5 us (24%)
  Pallas kernels  45.3 us (19%)
  starting transfers between devices  27.5 us (12%)
  between operations  14.2 us (6%)
  local copies, waits for them, and re-layouts  4.07 us (2%)
  other arithmetic  3 us (1%)
    all_to_all x3, blocking collectives, exchange(): lax.all_to_all(pieces, axis, 0, 0, tiled=True, axis_index_groups=index_gr...  55.4 us
    all_to_all x3, waiting for transfers between devices, exchange(): lax.all_to_all(pieces, axis, 0, 0, tiled=True, axis_index_groups=index_gr...  45.9 us
    pallas_call x1, Pallas kernels, inverse_factor(): pl.pallas_call(functools.partial(inverse_kernel, n, n_tp), out_shape=[jax...  30 us
    all_gather x1, blocking collectives, per_device(): basis_all = lax.all_gather(basis, 'fsdp', axis=1, tiled=True)  27.7 us
    all_to_all x3, starting transfers between devices, exchange(): lax.all_to_all(pieces, axis, 0, 0, tiled=True, axis_index_groups=index_gr...  16.3 us
    reduce_scatter x1, waiting for transfers between devices, per_device(): lax.psum_scatter(mine, 'fsdp', scatter_dimension=0, tiled=True, axis_inde...  9.22 us
    pallas_call x1, Pallas kernels, new_momentum(): pl.pallas_call(momentum_kernel, out_shape=[jax.ShapeDtypeStruct((rows, ra...  6.57 us
    pallas_call x1, Pallas kernels, project(): pl.pallas_call(functools.partial(right_kernel, chunk), out_shape=[jax.Sha...  6.23 us
  transfers between devices with their start and end apart: 7, of which 5 were waited for; matrix products, arithmetic and copies ran while one was open for 1% of the time, Pallas kernels for 15%

profile of v6, /device:TPU:1, one launch (start us, length us, event | category | flops | bytes accessed | tf_op | source)
XLA Modules:
  0.0 236.9 jit_solution(16917209285982860715)
XLA Ops:
  7.2 27.7 %all_gather.6 = bf16[448,1024]{0,1:T(8,128)(2,1)S(1)} all-gather(bf16[448,64]{0,1:T(8,128)(2,1)} %param.5), channel_id=1, replica_groups=mesh['fsdp'=16,'tp'=32] {'fsdp'}, dimensions={1}, use_global_device_ids=true | all-gather | bytes 974848 | tf_op jit(solution)/shard_map/all_gather | solution.py:446
  34.9 1.3 add_convert_fusion
  36.2 0.8 convolution_convert_fusion
  36.9 36.6 %all_to_all.30 = bf16[32,16,1024]{2,1,0:T(8,128)(2,1)S(1)} all-to-all(bf16[32,16,1024]{2,1,0:T(8,128)(2,1)S(1)} %bitcast.20), channel_id=1, replica_groups=mesh['fsdp'=16,'tp'=32] {'tp'}, dimensions={0} | all-to-all | bytes 2097152 | tf_op jit(solution)/shard_map/all_to_all | solution.py:27
  73.5 0.2 reduce_sum.39
  73.7 1.1 broadcast_in_dim.6
  74.8 5.9 %all-to-all-start.1 = ((bf16[32,16,1024]{2,1,0:T(8,128)(2,1)}), bf16[32,16,1024]{2,1,0:T(8,128)(2,1)S(1)}, u32[]{:S(2)}, u32[]{:S(2)}) async-start(bf16[32,16,1024]{2,1,0:T(8,128)(2,1)} %broadcast_in_dim.6), calls=%async_computation.1 | async-start | bytes 2097152 | tf_op jit(solution)/shard_map/all_to_all | solution.py:27
  80.6 0.0 reduce-scatter.2.cloned.1.call-start
  80.7 0.4 copy.8
  81.2 0.5 pad.4
  81.7 0.1 copy.10
  81.8 0.1 pad_add_fusion.place_ref
  81.8 24.4 %all-to-all-done.1 = bf16[32,16,1024]{2,1,0:T(8,128)(2,1)S(1)} async-done(((bf16[32,16,1024]{2,1,0:T(8,128)(2,1)}), bf16[32,16,1024]{2,1,0:T(8,128)(2,1)S(1)}, u32[]{:S(2)}, u32[]{:S(2)}) %all-to-all-start.1) | async-done | bytes 1048608 | tf_op jit(solution)/shard_map/all_to_all | solution.py:27
  106.3 0.0 copy-start
  106.3 2.5 %shard_map.58 = (f32[2,8,1152]{2,1,0:T(8,128)S(1)}, f32[256,1024]{1,0:T(8,128)S(1)}, f32[256,1024]{1,0:T(8,128)}) custom-call(s32[3]{0:T(128)S(1)} %pad_add_fusion.place_ref, bf16[512,1024]{1,0:T(8,128)(2,1)S(1)} %bitcast.15, bf16[512,512]{1,0:T(8,128)(2,1)S(1)} %bitcast.17), custom_call_target="tpu_custom_call" | custom-call | flops 805306368 | bytes 4194304 | tf_op jit(solution)/shard_map/pallas_call | solution.py:409
  108.8 5.3 %collective-permute-start = (f32[256,1024]{1,0:T(8,128)}, f32[256,1024]{1,0:T(8,128)S(1)}, u32[]{:S(2)}, u32[]{:S(2)}) collective-permute-start(f32[256,1024]{1,0:T(8,128)} %get-tuple-element.15), channel_id=1, source_target_pairs={{0,32},{32,0},{64,96},{96,64},{128,160},{160,128},{192,224},{224,1... | collective-permute-start | bytes 3145736 | tf_op jit(solution)/shard_map/ppermute | solution.py:462
  114.0 3.4 %all_to_all.31 = f32[2,8,1152]{2,1,0:T(8,128)S(1)} all-to-all(f32[2,8,1152]{2,1,0:T(8,128)S(1)} %get-tuple-element.14), channel_id=1, replica_groups={{0,32},{64,96},{128,160},{192,224},{256,288},{320,352},{384,416},{448,4..., dimensions={0} | all-to-all | bytes 147456 | tf_op jit(solution)/shard_map/all_to_all | solution.py:27
  117.5 0.0 collective-permute-done
  117.5 1.1 add.34
  118.6 0.0 copy-done
  118.6 0.0 reduce-scatter.2.cloned.1.call-update
  118.7 15.4 %all_to_all.32 = f32[8,8,1152]{2,1,0:T(8,128)S(1)} all-to-all(f32[8,8,1152]{2,1,0:T(8,128)S(1)} %broadcast_in_dim.7), channel_id=1, replica_groups={{0,64,128,192,256,320,384,448},{32,96,160,224,288,352,416,480},{1,65,12..., dimensions={0} | all-to-all | bytes 589824 | tf_op jit(solution)/shard_map/all_to_all | solution.py:27
  134.1 1.1 broadcast_in_dim.8
  135.2 5.1 %all-to-all-start.4 = ((f32[32,8,1152]{2,1,0:T(8,128)}), f32[32,8,1152]{2,1,0:T(8,128)S(1)}, u32[]{:S(2)}, u32[]{:S(2)}) async-start(f32[32,8,1152]{2,1,0:T(8,128)} %broadcast_in_dim.8), calls=%async_computation.4 | async-start | bytes 2359296 | tf_op jit(solution)/shard_map/all_to_all | solution.py:27
  140.3 0.0 all-gather.2.cloned.1.call-start
  140.4 9.2 %reduce-scatter.2.cloned.1.call-done = f32[32,1024]{1,0:T(8,128)} async-done(((f32[256,1024]{1,0:T(8,128)}), f32[32,1024]{1,0:T(8,128)}) %reduce-scatter.2.cloned.1.call-update) | async-done | bytes 131088 | tf_op jit(solution)/shard_map/reduce_scatter | solution.py:466
  149.6 0.0 all-gather.2.cloned.1.call-update
  149.6 18.8 %all-to-all-done.4.own_ref = f32[32,8,1152]{2,1,0:T(8,128)S(1)} async-done(((f32[32,8,1152]{2,1,0:T(8,128)}), f32[32,8,1152]{2,1,0:T(8,128)S(1)}, u32[]{:S(2)}, u32[]{:S(2)}) %all-to-all-start.4) | async-done | bytes 1179680 | tf_op jit(solution)/shard_map/all_to_all | solution.py:27
  168.4 5.8 %collective-permute-start.1 = (f32[32,8,1152]{2,1,0:T(8,128)S(1)}, f32[32,8,1152]{2,1,0:T(8,128)S(1)}, u32[]{:S(2)}, u32[]{:S(2)}) collective-permute-start(f32[32,8,1152]{2,1,0:T(8,128)S(1)} %all-to-all-done.4.own_ref), channel_id=1, source_target_pairs={{0,32},{32,0},{64,96},{96,64},{128,160},{160,128},{192,224},{224,1... | collective-permute-start | bytes 3538952 | tf_op jit(solution)/shard_map/ppermute | solution.py:473
  174.2 2.3 collective-permute-done.1.other_ref
  176.4 30.0 %shard_map.59 = (bf16[1024,1024]{1,0:T(8,128)(2,1)}, bf16[1024,1024]{1,0:T(8,128)(2,1)}) custom-call(s32[1]{0:T(128)} %bitcast.2.core_ref, f32[32,8,1152]{2,1,0:T(8,128)S(1)} %all-to-all-done.4.own_ref, f32[32,8,1152]{2,1,0:T(8,128)S(1)} %collective-permute-done.1.other_ref), custom_call_target="tpu_custom_call" | custom-call | flops 12884901888 | bytes 8388608 | tf_op jit(solution)/shard_map/pallas_call | solution.py:245
  206.4 0.0 all-gather.2.cloned.1.call-done.back_ref
  206.5 6.2 %shard_map.60 = (f32[448,1024]{1,0:T(8,128)}, f32[32,1,1024]{2,1,0:T(1,128)}) custom-call(f32[512,1024]{1,0:T(8,128)} %all-gather.2.cloned.1.call-done.back_ref, bf16[1024,1024]{1,0:T(8,128)(2,1)} %get-tuple-element.17.high_ref, bf16[1024,1024]{1,0:T(8,128)(2,1)} %get-tuple-element.18.low_ref), custom_call_target="tpu_custom_call" | custom-call | flops 2818572288 | bytes 3670016 | tf_op jit(solution)/shard_map/pallas_call | solution.py:303
  212.7 5.4 %all-to-all-start.5 = ((f32[32,1,1024]{2,1,0:T(1,128)}), f32[32,1,1024]{2,1,0:T(1,128)S(1)}, u32[]{:S(2)}, u32[]{:S(2)}) async-start(f32[32,1,1024]{2,1,0:T(1,128)} %get-tuple-element.23), calls=%async_computation.6 | async-start | bytes 262144 | tf_op jit(solution)/shard_map/all_to_all | solution.py:27
  218.1 0.0 copy-start.1
  218.1 6.6 %shard_map.61 = (bf16[512,1024]{1,0:T(8,128)(2,1)}, bf16[448,512]{1,0:T(8,128)(2,1)}) custom-call(bf16[512,1024]{1,0:T(8,128)(2,1)} %bitcast.16, bf16[1024,1024]{1,0:T(8,128)(2,1)} %get-tuple-element.17.high_ref, bf16[1024,1024]{1,0:T(8,128)(2,1)} %get-tuple-element.18.low_ref, f32[448,1024]{1,0:T(8,128)} %get-tuple-element.21.right_ref, ...), custom_call_target="tpu_custom_call" | custom-call | flops 2617245696 | bytes 5242880 | tf_op jit(solution)/shard_map/pallas_call | solution.py:353
  224.6 0.0 copy-start.2
  224.7 2.8 %all-to-all-done.5 = f32[32,1,1024]{2,1,0:T(1,128)S(1)} async-done(((f32[32,1,1024]{2,1,0:T(1,128)}), f32[32,1,1024]{2,1,0:T(1,128)S(1)}, u32[]{:S(2)}, u32[]{:S(2)}) %all-to-all-start.5) | async-done | bytes 131104 | tf_op jit(solution)/shard_map/all_to_all | solution.py:27
  227.4 0.1 reduce_sum.42
  227.5 0.0 copy-done.1
  227.5 0.2 divide_convert_fusion
  227.8 0.0 copy-done.2
  227.8 1.5 fusion
  229.2 0.1 constant_dynamic-slice_fusion
  229.3 0.7 copy.9
  (4 shorter events, 0.1 us)
Async XLA Ops:
  74.8 31.5 %all-to-all-start.1 = ((bf16[32,16,1024]{2,1,0:T(8,128)(2,1)}), bf16[32,16,1024]{2,1,0:T(8,128)(2,1)S(1)}, u32[]{:S(2)}, u32[]{:S(2)}) async-start(bf16[32,16,1024]{2,1,0:T(8,128)(2,1)} %broadcast_in_dim.6), calls=%async_computation.1 | async-start | bytes 2097152 | tf_op jit(solution)/shard_map/all_to_all | solution.py:27
  80.6 68.9 %reduce-scatter.2.cloned.1.call-start = ((), (), s32[]{:S(2)}) async-start(), calls=%async_computation.7 | async-start | bytes 1179648 | tf_op jit(solution)/shard_map/reduce_scatter | solution.py:466
  106.3 12.3 %copy-start = (bf16[32,16,1024]{2,1,0:T(8,128)(2,1)}, bf16[32,16,1024]{2,1,0:T(8,128)(2,1)S(1)}, u32[]{:S(2)}) copy-start(bf16[32,16,1024]{2,1,0:T(8,128)(2,1)S(1)} %all-to-all-done.1) | copy-start | bytes 3145732
  108.8 8.7 %collective-permute-start = (f32[256,1024]{1,0:T(8,128)}, f32[256,1024]{1,0:T(8,128)S(1)}, u32[]{:S(2)}, u32[]{:S(2)}) collective-permute-start(f32[256,1024]{1,0:T(8,128)} %get-tuple-element.15), channel_id=1, source_target_pairs={{0,32},{32,0},{64,96},{96,64},{128,160},{160,128},{192,224},{224,1... | collective-permute-start | bytes 3145736 | tf_op jit(solution)/shard_map/ppermute | solution.py:462
  135.2 33.2 %all-to-all-start.4 = ((f32[32,8,1152]{2,1,0:T(8,128)}), f32[32,8,1152]{2,1,0:T(8,128)S(1)}, u32[]{:S(2)}, u32[]{:S(2)}) async-start(f32[32,8,1152]{2,1,0:T(8,128)} %broadcast_in_dim.8), calls=%async_computation.4 | async-start | bytes 2359296 | tf_op jit(solution)/shard_map/all_to_all | solution.py:27
  140.3 66.1 %all-gather.2.cloned.1.call-start = ((), (), s32[]{:S(2)}) async-start(), calls=%async_computation.8 | async-start | bytes 2228224 | tf_op jit(solution)/shard_map/all_gather | solution.py:469
  168.4 8.1 %collective-permute-start.1 = (f32[32,8,1152]{2,1,0:T(8,128)S(1)}, f32[32,8,1152]{2,1,0:T(8,128)S(1)}, u32[]{:S(2)}, u32[]{:S(2)}) collective-permute-start(f32[32,8,1152]{2,1,0:T(8,128)S(1)} %all-to-all-done.4.own_ref), channel_id=1, source_target_pairs={{0,32},{32,0},{64,96},{96,64},{128,160},{160,128},{192,224},{224,1... | collective-permute-start | bytes 3538952 | tf_op jit(solution)/shard_map/ppermute | solution.py:473
  212.7 14.7 %all-to-all-start.5 = ((f32[32,1,1024]{2,1,0:T(1,128)}), f32[32,1,1024]{2,1,0:T(1,128)S(1)}, u32[]{:S(2)}, u32[]{:S(2)}) async-start(f32[32,1,1024]{2,1,0:T(1,128)} %get-tuple-element.23), calls=%async_computation.6 | async-start | bytes 262144 | tf_op jit(solution)/shard_map/all_to_all | solution.py:27
  218.1 9.5 %copy-start.1 = (f32[448,1024]{1,0:T(8,128)S(1)}, f32[448,1024]{1,0:T(8,128)}, u32[]{:S(2)}) copy-start(f32[448,1024]{1,0:T(8,128)} %get-tuple-element.21.right_ref) | copy-start | bytes 5505028
  224.6 3.1 %copy-start.2 = (bf16[512,1024]{1,0:T(8,128)(2,1)S(1)}, bf16[512,1024]{1,0:T(8,128)(2,1)}, u32[]{:S(2)}) copy-start(bf16[512,1024]{1,0:T(8,128)(2,1)} %get-tuple-element.24) | copy-start | bytes 3145732
Sparse Core Ops, SparseCore 0:
  118.8 30.7 reduce-scatter.1
  151.7 45.4 all-gather.1

commit v7 on v6

--- a/solution.py
+++ b/solution.py
@@ -185,6 +185,25 @@
             for p, (part, out) in enumerate(((high_ref, high_out), (low_ref, low_out)))
         ]
 
+    def pieces(j):
+        k = n_wide - 1
+        return [
+            pltpu.make_async_copy(
+                part.at[spans[k], spans[j]], out.at[spans[k], spans[j]], sems.at[p, k + j]
+            )
+            for p, (part, out) in enumerate(((high_ref, high_out), (low_ref, low_out)))
+        ]
+
+    def conclude(j):
+        k = n_wide - 1
+        if j < k:
+            advance(k, j)
+        high, low = split_parts(work[spans[k], spans[j]] * scale[:, spans[j]])
+        high_ref[spans[k], spans[j]] = high
+        low_ref[spans[k], spans[j]] = low
+        for copy in pieces(j):
+            copy.start()
+
     def finish(k):
         width = (k + 1) * wide
         high, low = split_parts(work[spans[k], :width] * scale[:, :width])
@@ -223,6 +242,9 @@
         if k + 1 < n_wide:
             advance(k, k + 1)
             take(k, k + 1, k + 1)
+        else:
+            aside += [functools.partial(conclude, j) for j in reversed(range(n_wide))]
+            continue
         others = [j for j in range(n_wide) if j not in (k, k + 1)]
         aside += [functools.partial(advance, k, j) for j in others]
         aside += [
@@ -234,8 +256,11 @@
         aside.append(functools.partial(finish, k))
     while aside:
         aside.pop(0)()
-    for k in range(n_wide):
+    for k in range(n_wide - 1):
         for copy in copies(k):
+            copy.wait()
+    for j in range(n_wide):
+        for copy in pieces(j):
             copy.wait()
 
 
@@ -255,7 +280,7 @@
             pltpu.VMEM((144, BLOCK), jnp.float32),
             pltpu.VMEM((rank, rank), jnp.bfloat16),
             pltpu.VMEM((rank, rank), jnp.bfloat16),
-            pltpu.SemaphoreType.DMA((2, n // 2)),
+            pltpu.SemaphoreType.DMA((2, n - 1)),
         ],
         compiler_params=pltpu.CompilerParams(vmem_limit_bytes=VM1),
         cost_estimate=pl.CostEstimate(
@@ -476,10 +501,13 @@
     inverse_high, inverse_low = inverse_factor(parity, own, other, rank)
     right, squares = project(back, inverse_high, inverse_low, cols, chunk, n_tp)
     squares = exchange(squares, "tp")
+    own_columns = lax.dynamic_slice_in_dim(right, me_fsdp * share, share, 1).T
+    own_columns = lax.optimization_barrier(own_columns)
     ortho_b, kept = new_momentum(left, inverse_high, inverse_low, right, momentum, grad)
     scale = jnp.sqrt(jnp.sum(squares, axis=(0, 1)) / cols_all + epsilon)
     basis_full = (right / scale[None, :]).astype(jnp.bfloat16)
-    basis_new = lax.dynamic_slice_in_dim(basis_full, me_fsdp * share, share, 1)
+    basis_new = (own_columns / lax.dynamic_slice_in_dim(scale, me_fsdp * share, share)[:, None]).T
+    basis_new = basis_new.astype(jnp.bfloat16)
     raw = dot(ortho_b, basis_full, by_cols)
     update = (math.sqrt(rows_all / rank) * raw).astype(jnp.bfloat16)
     return (kept.T, basis_new, update)

time: 237 us -> 238 us (level)
  no operation moved by 1% of the time
where the time goes in v7:
time: 238 us
  blocking collectives  83.1 us (35%)
  waiting for transfers between devices  56.4 us (24%)
  Pallas kernels  45.1 us (19%)
  starting transfers between devices  27.5 us (12%)
  between operations  14.2 us (6%)
  local copies, waits for them, and re-layouts  5.09 us (2%)
  matrix products  3.45 us (1%)
  other arithmetic  2.81 us (1%)
    all_to_all x3, blocking collectives, exchange(): lax.all_to_all(pieces, axis, 0, 0, tiled=True, axis_index_groups=index_gr...  55.4 us
    all_to_all x3, waiting for transfers between devices, exchange(): lax.all_to_all(pieces, axis, 0, 0, tiled=True, axis_index_groups=index_gr...  44.9 us
    pallas_call x1, Pallas kernels, inverse_factor(): pl.pallas_call(functools.partial(inverse_kernel, n, n_tp), out_shape=[jax...  29.8 us
    all_gather x1, blocking collectives, per_device(): basis_all = lax.all_gather(basis, 'fsdp', axis=1, tiled=True)  27.7 us
    all_to_all x3, starting transfers between devices, exchange(): lax.all_to_all(pieces, axis, 0, 0, tiled=True, axis_index_groups=index_gr...  16.4 us
    reduce_scatter x1, waiting for transfers between devices, per_device(): lax.psum_scatter(mine, 'fsdp', scatter_dimension=0, tiled=True, axis_inde...  9.23 us
    pallas_call x1, Pallas kernels, new_momentum(): pl.pallas_call(momentum_kernel, out_shape=[jax.ShapeDtypeStruct((rows, ra...  6.57 us
    pallas_call x1, Pallas kernels, project(): pl.pallas_call(functools.partial(right_kernel, chunk), out_shape=[jax.Sha...  6.25 us
  transfers between devices with their start and end apart: 7, of which 5 were waited for; matrix products, arithmetic and copies ran while one was open for 1% of the time, Pallas kernels for 15%

profile of v7, /device:TPU:1, one launch (start us, length us, event | category | flops | bytes accessed | tf_op | source)
XLA Modules:
  0.0 237.8 jit_solution(14058468771166872170)
XLA Ops:
  7.2 27.7 %all_gather.6 = bf16[448,1024]{0,1:T(8,128)(2,1)S(1)} all-gather(bf16[448,64]{0,1:T(8,128)(2,1)} %param.5), channel_id=1, replica_groups=mesh['fsdp'=16,'tp'=32] {'fsdp'}, dimensions={1}, use_global_device_ids=true | all-gather | bytes 974848 | tf_op jit(solution)/shard_map/all_gather | solution.py:471
  34.9 1.3 add_convert_fusion
  36.2 0.8 convolution_convert_fusion
  36.9 36.6 %all_to_all.30 = bf16[32,16,1024]{2,1,0:T(8,128)(2,1)S(1)} all-to-all(bf16[32,16,1024]{2,1,0:T(8,128)(2,1)S(1)} %bitcast.23), channel_id=1, replica_groups=mesh['fsdp'=16,'tp'=32] {'tp'}, dimensions={0} | all-to-all | bytes 2097152 | tf_op jit(solution)/shard_map/all_to_all | solution.py:27
  73.5 0.2 reduce_sum.39
  73.7 1.1 broadcast_in_dim.6
  74.8 5.9 %all-to-all-start.1 = ((bf16[32,16,1024]{2,1,0:T(8,128)(2,1)}), bf16[32,16,1024]{2,1,0:T(8,128)(2,1)S(1)}, u32[]{:S(2)}, u32[]{:S(2)}) async-start(bf16[32,16,1024]{2,1,0:T(8,128)(2,1)} %broadcast_in_dim.6), calls=%async_computation.1 | async-start | bytes 2097152 | tf_op jit(solution)/shard_map/all_to_all | solution.py:27
  80.6 0.0 reduce-scatter.2.cloned.1.call-start
  80.7 0.4 copy.8
  81.2 0.5 pad.4
  81.7 0.1 copy.10
  81.8 0.1 pad_add_fusion.place_ref
  81.8 24.4 %all-to-all-done.1 = bf16[32,16,1024]{2,1,0:T(8,128)(2,1)S(1)} async-done(((bf16[32,16,1024]{2,1,0:T(8,128)(2,1)}), bf16[32,16,1024]{2,1,0:T(8,128)(2,1)S(1)}, u32[]{:S(2)}, u32[]{:S(2)}) %all-to-all-start.1) | async-done | bytes 1048608 | tf_op jit(solution)/shard_map/all_to_all | solution.py:27
  106.3 0.0 copy-start
  106.3 2.5 %shard_map.58 = (f32[2,8,1152]{2,1,0:T(8,128)S(1)}, f32[256,1024]{1,0:T(8,128)S(1)}, f32[256,1024]{1,0:T(8,128)}) custom-call(s32[3]{0:T(128)S(1)} %pad_add_fusion.place_ref, bf16[512,1024]{1,0:T(8,128)(2,1)S(1)} %bitcast.18, bf16[512,512]{1,0:T(8,128)(2,1)S(1)} %bitcast.20), custom_call_target="tpu_custom_call" | custom-call | flops 805306368 | bytes 4194304 | tf_op jit(solution)/shard_map/pallas_call | solution.py:434
  108.8 5.3 %collective-permute-start = (f32[256,1024]{1,0:T(8,128)}, f32[256,1024]{1,0:T(8,128)S(1)}, u32[]{:S(2)}, u32[]{:S(2)}) collective-permute-start(f32[256,1024]{1,0:T(8,128)} %get-tuple-element.15), channel_id=1, source_target_pairs={{0,32},{32,0},{64,96},{96,64},{128,160},{160,128},{192,224},{224,1... | collective-permute-start | bytes 3145736 | tf_op jit(solution)/shard_map/ppermute | solution.py:487
  114.0 3.4 %all_to_all.31 = f32[2,8,1152]{2,1,0:T(8,128)S(1)} all-to-all(f32[2,8,1152]{2,1,0:T(8,128)S(1)} %get-tuple-element.14), channel_id=1, replica_groups={{0,32},{64,96},{128,160},{192,224},{256,288},{320,352},{384,416},{448,4..., dimensions={0} | all-to-all | bytes 147456 | tf_op jit(solution)/shard_map/all_to_all | solution.py:27
  117.5 0.0 collective-permute-done
  117.5 1.1 add.35
  118.6 0.0 copy-done
  118.6 0.0 reduce-scatter.2.cloned.1.call-update
  118.7 15.4 %all_to_all.32 = f32[8,8,1152]{2,1,0:T(8,128)S(1)} all-to-all(f32[8,8,1152]{2,1,0:T(8,128)S(1)} %broadcast_in_dim.7), channel_id=1, replica_groups={{0,64,128,192,256,320,384,448},{32,96,160,224,288,352,416,480},{1,65,12..., dimensions={0} | all-to-all | bytes 589824 | tf_op jit(solution)/shard_map/all_to_all | solution.py:27
  134.1 1.1 broadcast_in_dim.8
  135.2 5.1 %all-to-all-start.4 = ((f32[32,8,1152]{2,1,0:T(8,128)}), f32[32,8,1152]{2,1,0:T(8,128)S(1)}, u32[]{:S(2)}, u32[]{:S(2)}) async-start(f32[32,8,1152]{2,1,0:T(8,128)} %broadcast_in_dim.8), calls=%async_computation.4 | async-start | bytes 2359296 | tf_op jit(solution)/shard_map/all_to_all | solution.py:27
  140.3 0.0 all-gather.2.cloned.1.call-start
  140.4 9.2 %reduce-scatter.2.cloned.1.call-done = f32[32,1024]{1,0:T(8,128)} async-done(((f32[256,1024]{1,0:T(8,128)}), f32[32,1024]{1,0:T(8,128)}) %reduce-scatter.2.cloned.1.call-update) | async-done | bytes 131088 | tf_op jit(solution)/shard_map/reduce_scatter | solution.py:491
  149.6 0.0 all-gather.2.cloned.1.call-update
  149.7 18.7 %all-to-all-done.4.own_ref = f32[32,8,1152]{2,1,0:T(8,128)S(1)} async-done(((f32[32,8,1152]{2,1,0:T(8,128)}), f32[32,8,1152]{2,1,0:T(8,128)S(1)}, u32[]{:S(2)}, u32[]{:S(2)}) %all-to-all-start.4) | async-done | bytes 1179680 | tf_op jit(solution)/shard_map/all_to_all | solution.py:27
  168.4 5.8 %collective-permute-start.1 = (f32[32,8,1152]{2,1,0:T(8,128)S(1)}, f32[32,8,1152]{2,1,0:T(8,128)S(1)}, u32[]{:S(2)}, u32[]{:S(2)}) collective-permute-start(f32[32,8,1152]{2,1,0:T(8,128)S(1)} %all-to-all-done.4.own_ref), channel_id=1, source_target_pairs={{0,32},{32,0},{64,96},{96,64},{128,160},{160,128},{192,224},{224,1... | collective-permute-start | bytes 3538952 | tf_op jit(solution)/shard_map/ppermute | solution.py:498
  174.2 2.3 collective-permute-done.1.other_ref
  176.5 29.8 %shard_map.59 = (bf16[1024,1024]{1,0:T(8,128)(2,1)}, bf16[1024,1024]{1,0:T(8,128)(2,1)}) custom-call(s32[1]{0:T(128)} %bitcast.2.core_ref, f32[32,8,1152]{2,1,0:T(8,128)S(1)} %all-to-all-done.4.own_ref, f32[32,8,1152]{2,1,0:T(8,128)S(1)} %collective-permute-done.1.other_ref), custom_call_target="tpu_custom_call" | custom-call | flops 12884901888 | bytes 8388608 | tf_op jit(solution)/shard_map/pallas_call | solution.py:270
  206.3 0.0 all-gather.2.cloned.1.call-done.back_ref
  206.3 6.2 %shard_map.60 = (f32[448,1024]{1,0:T(8,128)}, f32[32,1,1024]{2,1,0:T(1,128)}) custom-call(f32[512,1024]{1,0:T(8,128)} %all-gather.2.cloned.1.call-done.back_ref, bf16[1024,1024]{1,0:T(8,128)(2,1)} %get-tuple-element.17.high_ref, bf16[1024,1024]{1,0:T(8,128)(2,1)} %get-tuple-element.18.low_ref), custom_call_target="tpu_custom_call" | custom-call | flops 2818572288 | bytes 3670016 | tf_op jit(solution)/shard_map/pallas_call | solution.py:328
  212.6 5.4 %all-to-all-start.5 = ((f32[32,1,1024]{2,1,0:T(1,128)}), f32[32,1,1024]{2,1,0:T(1,128)S(1)}, u32[]{:S(2)}, u32[]{:S(2)}) async-start(f32[32,1,1024]{2,1,0:T(1,128)} %get-tuple-element.23), calls=%async_computation.6 | async-start | bytes 262144 | tf_op jit(solution)/shard_map/all_to_all | solution.py:27
  218.0 1.1 dynamic-slice_bitcast_fusion
  219.0 0.0 copy-start.1
  219.0 6.6 %shard_map.61 = (bf16[512,1024]{1,0:T(8,128)(2,1)}, bf16[448,512]{1,0:T(8,128)(2,1)}) custom-call(bf16[512,1024]{1,0:T(8,128)(2,1)} %bitcast.19, bf16[1024,1024]{1,0:T(8,128)(2,1)} %get-tuple-element.17.high_ref, bf16[1024,1024]{1,0:T(8,128)(2,1)} %get-tuple-element.18.low_ref, f32[448,1024]{1,0:T(8,128)} %get-tuple-element.21.right_ref, ...), custom_call_target="tpu_custom_call" | custom-call | flops 2617245696 | bytes 5242880 | tf_op jit(solution)/shard_map/pallas_call | solution.py:378
  225.6 1.7 all-to-all-done.5
  227.3 0.1 reduce_sum.42
  227.4 0.1 dynamic_slice.7
  227.5 0.0 copy-done.1
  227.5 2.7 %fusion = bf16[512,448]{0,1:T(8,128)(2,1)} fusion(bf16[512,1024]{1,0:T(8,128)(2,1)} %get-tuple-element.24, f32[448,1024]{1,0:T(8,128)S(1)} %copy-done.1, f32[1024]{0:T(1024)S(1)} %add_sqrt_fusion), kind=kOutput, calls=%fused_computation.3 | convolution fusion | flops 471138304 | bytes 3346432 | tf_op jit(solution)/shard_map/dot_general | solution.py:467
  230.2 0.7 copy.9
  (5 shorter events, 0.1 us)
Async XLA Ops:
  74.8 31.5 %all-to-all-start.1 = ((bf16[32,16,1024]{2,1,0:T(8,128)(2,1)}), bf16[32,16,1024]{2,1,0:T(8,128)(2,1)S(1)}, u32[]{:S(2)}, u32[]{:S(2)}) async-start(bf16[32,16,1024]{2,1,0:T(8,128)(2,1)} %broadcast_in_dim.6), calls=%async_computation.1 | async-start | bytes 2097152 | tf_op jit(solution)/shard_map/all_to_all | solution.py:27
  80.6 69.0 %reduce-scatter.2.cloned.1.call-start = ((), (), s32[]{:S(2)}) async-start(), calls=%async_computation.7 | async-start | bytes 1179648 | tf_op jit(solution)/shard_map/reduce_scatter | solution.py:491
  106.3 12.3 %copy-start = (bf16[32,16,1024]{2,1,0:T(8,128)(2,1)}, bf16[32,16,1024]{2,1,0:T(8,128)(2,1)S(1)}, u32[]{:S(2)}) copy-start(bf16[32,16,1024]{2,1,0:T(8,128)(2,1)S(1)} %all-to-all-done.1) | copy-start | bytes 3145732
  108.8 8.7 %collective-permute-start = (f32[256,1024]{1,0:T(8,128)}, f32[256,1024]{1,0:T(8,128)S(1)}, u32[]{:S(2)}, u32[]{:S(2)}) collective-permute-start(f32[256,1024]{1,0:T(8,128)} %get-tuple-element.15), channel_id=1, source_target_pairs={{0,32},{32,0},{64,96},{96,64},{128,160},{160,128},{192,224},{224,1... | collective-permute-start | bytes 3145736 | tf_op jit(solution)/shard_map/ppermute | solution.py:487
  135.2 33.2 %all-to-all-start.4 = ((f32[32,8,1152]{2,1,0:T(8,128)}), f32[32,8,1152]{2,1,0:T(8,128)S(1)}, u32[]{:S(2)}, u32[]{:S(2)}) async-start(f32[32,8,1152]{2,1,0:T(8,128)} %broadcast_in_dim.8), calls=%async_computation.4 | async-start | bytes 2359296 | tf_op jit(solution)/shard_map/all_to_all | solution.py:27
  140.3 66.0 %all-gather.2.cloned.1.call-start = ((), (), s32[]{:S(2)}) async-start(), calls=%async_computation.8 | async-start | bytes 2228224 | tf_op jit(solution)/shard_map/all_gather | solution.py:494
  168.4 8.1 %collective-permute-start.1 = (f32[32,8,1152]{2,1,0:T(8,128)S(1)}, f32[32,8,1152]{2,1,0:T(8,128)S(1)}, u32[]{:S(2)}, u32[]{:S(2)}) collective-permute-start(f32[32,8,1152]{2,1,0:T(8,128)S(1)} %all-to-all-done.4.own_ref), channel_id=1, source_target_pairs={{0,32},{32,0},{64,96},{96,64},{128,160},{160,128},{192,224},{224,1... | collective-permute-start | bytes 3538952 | tf_op jit(solution)/shard_map/ppermute | solution.py:498
  212.6 14.7 %all-to-all-start.5 = ((f32[32,1,1024]{2,1,0:T(1,128)}), f32[32,1,1024]{2,1,0:T(1,128)S(1)}, u32[]{:S(2)}, u32[]{:S(2)}) async-start(f32[32,1,1024]{2,1,0:T(1,128)} %get-tuple-element.23), calls=%async_computation.6 | async-start | bytes 262144 | tf_op jit(solution)/shard_map/all_to_all | solution.py:27
  219.0 8.5 %copy-start.1 = (f32[448,1024]{1,0:T(8,128)S(1)}, f32[448,1024]{1,0:T(8,128)}, u32[]{:S(2)}) copy-start(f32[448,1024]{1,0:T(8,128)} %get-tuple-element.21.right_ref) | copy-start | bytes 5505028
Sparse Core Ops, SparseCore 0:
  118.8 30.8 reduce-scatter.1
  151.7 45.4 all-gather.1
